TPU v7x, 32 devices: a whole 2x2x4 slice. The times are simulated.
32 devices in a mesh: dp: 4 (over z), ctx: 2 (over x), tp: 4 (over y, core).
Axes of the slice: x: 2, y: 2, z: 4, core: 2. Of those that a mesh axis runs over, the one named last changes fastest.
Arguments:
- tokens: bfloat16 [8192, 1024], P(('dp', 'ctx')), may hold values from -6 to 6
- cotangent: bfloat16 [8192, 1024], P(('dp', 'ctx')), may hold values from -6 to 6
- lengths: int32 [4, 4], P('dp'), may hold values from 1 to 2048, as said below
- norm1_gain: float32 [1024], replicated, may hold values from 0.5 to 1.5
- norm2_gain: float32 [1024], replicated, may hold values from 0.5 to 1.5
- query_proj: bfloat16 [1024, 512], P(('dp', 'ctx'), 'tp'), may hold values from -0.1875 to 0.1875
- keyval_proj: bfloat16 [1024, 2, 128], P(('dp', 'ctx')), may hold values from -0.1875 to 0.1875
- attn_proj: bfloat16 [512, 1024], P('tp', ('dp', 'ctx')), may hold values from -1 to 1
- inner_proj: bfloat16 [1024, 2, 1536], P(('dp', 'ctx'), None, 'tp'), may hold values from -0.1875 to 0.1875
- state_proj: bfloat16 [1024, 2, 128], P(('dp', 'ctx')), may hold values from -0.1875 to 0.1875
- step_proj: bfloat16 [1024, 24], P(('dp', 'ctx'), 'tp'), may hold values from -0.1875 to 0.1875
- conv_inner: float32 [5, 1536], replicated, may hold values from -3 to 3
- conv_state: float32 [5, 2, 128], replicated, may hold values from -3 to 3
- step_bias: float32 [24], replicated, may hold values from -9 to -2
- decay_log: float32 [24], replicated, may hold values from -1 to 1
- skip_gain: float32 [24], replicated, may hold values from 0.5 to 1.5
- mamba_gain: float32 [1536], replicated, may hold values from 0.5 to 1.5
- mamba_proj: bfloat16 [1536, 1024], P('tp', ('dp', 'ctx')), may hold values from -0.15625 to 0.15625
- gateup_proj: bfloat16 [1024, 2, 2048], P(('dp', 'ctx'), None, 'tp'), may hold values from -0.1875 to 0.1875
- down_proj: bfloat16 [2048, 1024], P('tp', ('dp', 'ctx')), may hold values from -0.125 to 0.125
Outputs:
- layer_out: bfloat16 [8192, 1024], P(('dp', 'ctx'))
- tokens_grad: bfloat16 [8192, 1024], P(('dp', 'ctx'))
- norm1_grad: float32 [1024], replicated
- norm2_grad: float32 [1024], replicated
- query_grad: float32 [1024, 512], P(('dp', 'ctx'), 'tp')
- keyval_grad: float32 [1024, 2, 128], P(('dp', 'ctx'))
- attn_grad: float32 [512, 1024], P('tp', ('dp', 'ctx'))
- inner_grad: float32 [1024, 2, 1536], P(('dp', 'ctx'), None, 'tp')
- state_grad: float32 [1024, 2, 128], P(('dp', 'ctx'))
- step_grad: float32 [1024, 24], P(('dp', 'ctx'), 'tp')
- convin_grad: float32 [5, 1536], replicated
- convst_grad: float32 [5, 2, 128], replicated
- stepbias_grad: float32 [24], replicated
- decay_grad: float32 [24], replicated
- skip_grad: float32 [24], replicated
- mgain_grad: float32 [1536], replicated
- mamba_grad: float32 [1536, 1024], P('tp', ('dp', 'ctx'))
- gateup_grad: float32 [1024, 2, 2048], P(('dp', 'ctx'), None, 'tp')
- down_grad: float32 [2048, 1024], P('tp', ('dp', 'ctx'))
Inputs may be any that keep to these rules, and one draw needn't show every extreme that they name: Row r lists, in order, the lengths of the 4 documents packed into the 2048 tokens of dp index r; each row sums to 2048.
All inputs are finite; a program needn't handle non-finite values.
Results may differ from a plain program's by a relative error of at most 0.03.
Values may be sent and summed in bfloat16 or wider, within the bound.
No kernel may reach another device: no remote copies, remote signals or barrier semaphores. Data moves between devices by JAX's collectives and lax.ppermute only.
A program may use at most 192 MiB of HBM per device.

v0:
```python
import jax
import jax.numpy as jnp
from jax import lax
from jax.sharding import PartitionSpec as P

H = 8
KVH = 2
HD = 64
NST = 128
CONV = 4
SCAN_BLOCK = 256
KEY_BLOCK = 512


EPS = 1e-05
ROPE_BASE = 10000.0
MASKED = -1e30
HIGH = lax.Precision.HIGHEST


def passed_along(value, axis, steps):
    count = lax.axis_size(axis)
    leading, last = (max(0, -steps), min(count, count - steps))
    return lax.ppermute(value, axis, [(source, source + steps) for source in range(leading, last)])


def carried_in_2(shard, axis, combine, identity):
    peers, mine = (lax.axis_size(axis), lax.axis_index(axis))
    everything = jax.tree.map(
        lambda part, kind: lax.all_gather(part.astype(kind), axis),
        shard,
        (jnp.bfloat16, jnp.bfloat16),
    )
    start = jax.tree.map(
        lambda part, zero: jnp.broadcast_to(jnp.asarray(zero, part.dtype), part.shape),
        shard,
        identity,
    )

    def hop(k, before):
        reached = k < mine
        new = combine(
            before, jax.tree.map(lambda part, own: part[k].astype(own.dtype), everything, shard)
        )
        return jax.tree.map(lambda a, b: jnp.where(reached, a, b), new, before)

    return lax.fori_loop(0, peers, hop, start)


def prefix_2(shard, axis, join, neutral):
    count = lax.axis_size(axis)
    place = lax.axis_index(axis)
    ahead = count - 1 - place
    gathered = jax.tree.map(
        lambda a, kind: lax.all_gather(a.astype(kind), axis),
        shard,
        jax.tree.map(lambda a: jnp.bfloat16 if a.dtype == jnp.float32 else a.dtype, shard),
    )
    state = jax.tree.map(lambda a, e: jnp.zeros_like(a) + jnp.asarray(e, a.dtype), shard, neutral)

    def one(hop, state):
        source = count - 1 - hop
        return join(
            state,
            jax.tree.map(
                lambda a, own: lax.dynamic_index_in_dim(a, source, 0, False).astype(own.dtype),
                gathered,
                shard,
            ),
        )

    return lax.fori_loop(0, ahead, one, state)


def product(left, right):
    return jnp.dot(left, right, preferred_element_type=jnp.float32)


def product_tn(left, right):
    return lax.dot_general(
        left, right, (((0,), (0,)), ((), ())), preferred_element_type=jnp.float32
    )


def product_nt(left, right):
    return lax.dot_general(
        left, right, (((1,), (1,)), ((), ())), preferred_element_type=jnp.float32
    )


def rms_scale(values, gain):
    return values * lax.rsqrt(jnp.mean(values * values, axis=-1, keepdims=True) + EPS) * gain


def rope_turn(values, rel_pos):
    half_dim = values.shape[-1] // 2
    frequency = ROPE_BASE ** (-jnp.arange(half_dim, dtype=jnp.float32) / half_dim)
    angles = rel_pos.astype(jnp.float32)[:, None] * frequency[None, :]
    cosine = jnp.cos(angles)[:, None, :]
    sine_part = jnp.sin(angles)[:, None, :]
    first_half = values[..., :half_dim]
    second = values[..., half_dim:]
    return jnp.concatenate(
        [first_half * cosine - second * sine_part, second * cosine + first_half * sine_part],
        axis=-1,
    )


def doc_layout(doc_lengths, positions):
    bounds = jnp.cumsum(doc_lengths)
    doc_ids = jnp.sum((positions[:, None] >= bounds[None, :]).astype(jnp.int32), axis=1)
    starts = bounds - doc_lengths
    member = doc_ids[:, None] == jnp.arange(bounds.shape[0], dtype=jnp.int32)[None, :]
    doc_start = jnp.sum(jnp.where(member, starts[None, :], 0), axis=1)
    return (doc_ids, positions - doc_start)


def causal_conv(extended, taps, rel_pos):
    width = taps.shape[0] - 1
    row_count = rel_pos.shape[0]
    summed = taps[width]
    for lag_steps in range(width):
        shifted = extended[width - 1 - lag_steps : width - 1 - lag_steps + row_count]
        summed = (
            summed
            + taps[width - 1 - lag_steps]
            * shifted
            * (rel_pos >= lag_steps).astype(jnp.float32)[:, None]
        )
    return jax.nn.silu(summed)


def scan_block(carried_in, block_in):
    state_now, state_doc = carried_in
    inner_vals, step_size, log_decay, write_vec, read_vec, doc_ids = block_in
    cumulative = jnp.cumsum(log_decay, axis=0)
    order_idx = jnp.arange(doc_ids.shape[0], dtype=jnp.int32)
    linked = (doc_ids[:, None] == doc_ids[None, :]) & (order_idx[:, None] >= order_idx[None, :])
    weights = jnp.exp(
        jnp.where(linked[:, :, None], cumulative[:, None, :] - cumulative[None, :, :], MASKED)
    )
    couple = jnp.dot(read_vec, write_vec.T, precision=HIGH)
    mixing = couple[:, :, None] * weights * step_size[None, :, :]
    within = jnp.einsum("tsh,shp->thp", mixing, inner_vals, precision=HIGH)
    inflow = (doc_ids == state_doc).astype(jnp.float32)[:, None] * jnp.exp(cumulative)
    carried = jnp.einsum("tn,hpn->thp", read_vec, state_now, precision=HIGH) * inflow[:, :, None]
    last_doc = doc_ids[-1]
    tail_weight = (
        jnp.where(
            (doc_ids == last_doc)[:, None], jnp.exp(cumulative[-1][None, :] - cumulative), 0.0
        )
        * step_size
    )
    kept_part = jnp.where(state_doc == last_doc, jnp.exp(cumulative[-1]), 0.0)
    new_state = kept_part[:, None, None] * state_now + jnp.einsum(
        "sh,shp,sn->hpn", tail_weight, inner_vals, write_vec, precision=HIGH
    )
    return ((new_state, last_doc), within + carried)


def state_scan(inner_vals, step_size, log_decay, write_vec, read_vec, doc_ids, block_len):
    pieces = inner_vals.shape[0] // block_len

    def split_rows(values):
        return values.reshape((pieces, block_len) + values.shape[1:])

    start_state = jnp.zeros(
        (inner_vals.shape[1], inner_vals.shape[2], write_vec.shape[1]), jnp.float32
    )
    blocks_in = (
        split_rows(inner_vals),
        split_rows(step_size),
        split_rows(log_decay),
        split_rows(write_vec),
        split_rows(read_vec),
        split_rows(doc_ids),
    )
    final_pair, outputs = lax.scan(
        jax.checkpoint(scan_block), (start_state, jnp.array(-1, jnp.int32)), blocks_in
    )
    return (outputs.reshape(inner_vals.shape), final_pair[0])


def chain_step(earlier, later):
    return (earlier[0] * later[0], later[0][:, None, None] * earlier[1] + later[1])


def body(
    tokens,
    cotangent,
    lengths,
    norm1_gain,
    norm2_gain,
    query_proj,
    keyval_proj,
    attn_proj,
    inner_proj,
    state_proj,
    step_proj,
    conv_inner,
    conv_state,
    step_bias,
    decay_log,
    skip_gain,
    mamba_gain,
    mamba_proj,
    gateup_proj,
    down_proj,
):
    query_w, keyval_w, attn_w, inner_w, state_w, step_w, mamba_w, gateup_w, down_w = (
        lax.all_gather(query_proj, ("dp", "ctx"), axis=0, tiled=True),
        lax.all_gather(keyval_proj, ("dp", "ctx"), axis=0, tiled=True),
        lax.all_gather(attn_proj, ("dp", "ctx"), axis=1, tiled=True),
        lax.all_gather(inner_proj, ("dp", "ctx"), axis=0, tiled=True),
        lax.all_gather(state_proj, ("dp", "ctx"), axis=0, tiled=True),
        lax.all_gather(step_proj, ("dp", "ctx"), axis=0, tiled=True),
        lax.all_gather(mamba_proj, ("dp", "ctx"), axis=1, tiled=True),
        lax.all_gather(gateup_proj, ("dp", "ctx"), axis=0, tiled=True),
        lax.all_gather(down_proj, ("dp", "ctx"), axis=1, tiled=True),
    )
    row_count = tokens.shape[0]
    tensor_rank = lax.axis_index("tp")
    tensor_size = lax.axis_size("tp")
    ctx_rank = lax.axis_index("ctx")
    pack_len = row_count * lax.axis_size("ctx")
    heads_local = query_w.shape[1] // HD
    mamba_heads = step_w.shape[1]
    inner_width = inner_w.shape[2]
    ff_width = gateup_w.shape[2]
    score_scale = HD ** (-0.5)
    kv_head = tensor_rank * heads_local // (H // KVH)
    key_blocks = pack_len // KEY_BLOCK
    doc_lengths = lengths[0]
    first_row = ctx_rank * row_count
    needed_blocks = (first_row + row_count) // KEY_BLOCK
    positions = first_row + jnp.arange(row_count, dtype=jnp.int32)
    doc_ids, rel_pos = doc_layout(doc_lengths, positions)
    key_docs, _key_rel = doc_layout(doc_lengths, jnp.arange(pack_len, dtype=jnp.int32))
    before_doc, _before_rel = doc_layout(
        doc_lengths, jnp.reshape(jnp.maximum(first_row - 1, 0), (1,))
    )
    prev_doc = jnp.where(first_row > 0, before_doc[0], -1)
    hidden_in = tokens.astype(jnp.float32)
    normed = rms_scale(hidden_in, norm1_gain).astype(jnp.bfloat16)
    queries = product(normed, query_w).reshape(row_count, heads_local, HD)
    q_rot = rope_turn(queries, rel_pos).astype(jnp.bfloat16)
    keyval_mine = lax.dynamic_slice_in_dim(keyval_w, kv_head * HD, HD, 2)
    keyval = product(normed, keyval_mine.reshape(keyval_mine.shape[0], 2 * HD))
    key_pre = keyval[:, None, :HD]
    k_rot = rope_turn(key_pre, rel_pos)[:, 0]
    kv_local = jnp.concatenate([k_rot, keyval[:, HD:]], axis=1).astype(jnp.bfloat16)
    kv_all = lax.all_gather(kv_local, "ctx", axis=0, tiled=True)

    def block_scores(block_start):
        block_rows = lax.dynamic_slice_in_dim(kv_all, block_start, KEY_BLOCK, 0)
        keys_blk = block_rows[:, :HD]
        values_blk = block_rows[:, HD:]
        raw_scores = (
            jnp.einsum("qhd,kd->hqk", q_rot, keys_blk, preferred_element_type=jnp.float32)
            * score_scale
        )
        docs_blk = lax.dynamic_slice_in_dim(key_docs, block_start, KEY_BLOCK, 0)
        pos_blk = block_start + jnp.arange(KEY_BLOCK, dtype=jnp.int32)
        allowed = (doc_ids[:, None] == docs_blk[None, :]) & (pos_blk[None, :] <= positions[:, None])
        return (jnp.where(allowed[None], raw_scores, MASKED), keys_blk, values_blk)

    def max_step(block_idx, stats):
        run_max, run_total = stats
        scores, _keys, _values = block_scores(block_idx * KEY_BLOCK)
        new_max = jnp.maximum(run_max, jnp.max(scores, axis=-1))
        run_total = run_total * jnp.exp(run_max - new_max) + jnp.sum(
            jnp.exp(scores - new_max[:, :, None]), axis=-1
        )
        return (new_max, run_total)

    start_stats = (
        jnp.full((heads_local, row_count), MASKED, jnp.float32),
        jnp.zeros((heads_local, row_count), jnp.float32),
    )
    row_max, row_total = lax.fori_loop(0, needed_blocks, max_step, start_stats)
    log_total = row_max + jnp.log(row_total)

    def value_step(block_idx, summed):
        scores, _keys, values_blk = block_scores(block_idx * KEY_BLOCK)
        probs = jnp.exp(scores - log_total[:, :, None]).astype(jnp.bfloat16)
        return summed + jnp.einsum(
            "hqk,kd->qhd", probs, values_blk, preferred_element_type=jnp.float32
        )

    attended = lax.fori_loop(
        0, needed_blocks, value_step, jnp.zeros((row_count, heads_local, HD), jnp.float32)
    )
    attended_low = attended.reshape(row_count, heads_local * HD).astype(jnp.bfloat16)
    attn_part = product(attended_low, attn_w)
    inner_all = product(normed, inner_w.reshape(inner_w.shape[0], -1))
    gate_z = inner_all[:, :inner_width]
    state_all = product(normed, state_w.reshape(state_w.shape[0], -1))
    step_raw = product(normed, step_w)
    mixed_in = jnp.concatenate([inner_all[:, inner_width:], state_all], axis=1).astype(jnp.bfloat16)
    edge_rows = passed_along(mixed_in[row_count - (CONV - 1) :], "ctx", 1)
    extended = jnp.concatenate([edge_rows, mixed_in], axis=0).astype(jnp.float32)
    channel_start = tensor_rank * inner_width
    head_start = tensor_rank * mamba_heads
    taps = jnp.concatenate(
        [
            lax.dynamic_slice_in_dim(conv_inner, channel_start, inner_width, 1),
            conv_state.reshape(conv_state.shape[0], -1),
        ],
        axis=1,
    )
    bias_local = lax.dynamic_slice_in_dim(step_bias, head_start, mamba_heads, 0)
    decay_local = lax.dynamic_slice_in_dim(decay_log, head_start, mamba_heads, 0)
    skip_local = lax.dynamic_slice_in_dim(skip_gain, head_start, mamba_heads, 0)
    gain_local = lax.dynamic_slice_in_dim(mamba_gain, channel_start, inner_width, 0)

    def prepare(extended_in, step_in, taps_in, bias_in, decay_in):
        activated = causal_conv(extended_in, taps_in, rel_pos)
        inner_vals = activated[:, :inner_width].reshape(row_count, mamba_heads, -1)
        write_vec = activated[:, inner_width : inner_width + NST]
        read_vec = activated[:, inner_width + NST :]
        step_size = jax.nn.softplus(step_in + bias_in)
        log_decay = -step_size * jnp.exp(decay_in)
        return (inner_vals, step_size, log_decay, write_vec, read_vec)

    def local_states(inner_vals, step_size, log_decay, write_vec, read_vec):
        ssm_local, end_state = state_scan(
            inner_vals, step_size, log_decay, write_vec, read_vec, doc_ids, SCAN_BLOCK
        )
        through = jnp.where(prev_doc == doc_ids[-1], jnp.exp(jnp.sum(log_decay, axis=0)), 0.0)
        return (ssm_local, end_state, through)

    def incoming(read_vec, log_decay, state_in):
        cumulative = jnp.cumsum(log_decay, axis=0)
        inflow = (doc_ids == prev_doc).astype(jnp.float32)[:, None] * jnp.exp(cumulative)
        return jnp.einsum("tn,hpn->thp", read_vec, state_in, precision=HIGH) * inflow[:, :, None]

    def finish(ssm_out, inner_vals, gate_in, skip_in, gain_in):
        with_skip = ssm_out + skip_in[None, :, None] * inner_vals
        gated = with_skip * jax.nn.silu(gate_in).reshape(with_skip.shape)
        normed_heads = (
            gated
            * lax.rsqrt(jnp.mean(gated * gated, axis=-1, keepdims=True) + EPS)
            * gain_in.reshape(with_skip.shape[1:])
        )
        return normed_heads.reshape(row_count, -1)

    inner_vals, step_size, log_decay, write_vec, read_vec = prepare(
        extended, step_raw, taps, bias_local, decay_local
    )
    ssm_local, end_state, through = local_states(
        inner_vals, step_size, log_decay, write_vec, read_vec
    )
    identity_pair = (jnp.ones((mamba_heads,), jnp.float32), jnp.zeros_like(end_state))
    prefix = carried_in_2((through, end_state), "ctx", chain_step, identity_pair)
    state_in = prefix[1]
    ssm_out = ssm_local + incoming(read_vec, log_decay, state_in)
    mamba_low = finish(ssm_out, inner_vals, gate_z, skip_local, gain_local).astype(jnp.bfloat16)
    mamba_part = product(mamba_low, mamba_w)
    mixer_sum = lax.psum((attn_part + mamba_part).astype(jnp.bfloat16), "tp").astype(jnp.float32)
    residual = hidden_in + mixer_sum
    normed2 = rms_scale(residual, norm2_gain).astype(jnp.bfloat16)
    gateup = product(normed2, gateup_w.reshape(gateup_w.shape[0], -1))

    def activate(gateup_in):
        return jax.nn.silu(gateup_in[:, :ff_width]) * gateup_in[:, ff_width:]

    hidden_act = activate(gateup).astype(jnp.bfloat16)
    mlp_sum = lax.psum(product(hidden_act, down_w).astype(jnp.bfloat16), "tp").astype(jnp.float32)
    layer_out = (residual + mlp_sum).astype(jnp.bfloat16)
    query_w, keyval_w, attn_w, inner_w, state_w, step_w, mamba_w, gateup_w, down_w = (
        lax.all_gather(query_proj, ("dp", "ctx"), axis=0, tiled=True),
        lax.all_gather(keyval_proj, ("dp", "ctx"), axis=0, tiled=True),
        lax.all_gather(attn_proj, ("dp", "ctx"), axis=1, tiled=True),
        lax.all_gather(inner_proj, ("dp", "ctx"), axis=0, tiled=True),
        lax.all_gather(state_proj, ("dp", "ctx"), axis=0, tiled=True),
        lax.all_gather(step_proj, ("dp", "ctx"), axis=0, tiled=True),
        lax.all_gather(mamba_proj, ("dp", "ctx"), axis=1, tiled=True),
        lax.all_gather(gateup_proj, ("dp", "ctx"), axis=0, tiled=True),
        lax.all_gather(down_proj, ("dp", "ctx"), axis=1, tiled=True),
    )
    quarter = row_count // tensor_size

    def gain_part(values, grad_normed):
        values_q = lax.dynamic_slice_in_dim(values, tensor_rank * quarter, quarter, 0)
        grad_q = lax.dynamic_slice_in_dim(grad_normed, tensor_rank * quarter, quarter, 0)
        unit_rows = values_q * lax.rsqrt(
            jnp.mean(values_q * values_q, axis=-1, keepdims=True) + EPS
        )
        return jnp.sum(grad_q * unit_rows, axis=0)

    grad_hidden = product_nt(cotangent, down_w)
    down_grad = product_tn(hidden_act, cotangent)
    _act_value, act_pull = jax.vjp(activate, gateup)
    grad_gateup = act_pull(grad_hidden)[0].astype(jnp.bfloat16)
    gateup_grad = product_tn(normed2, grad_gateup).reshape(gateup_w.shape)
    grad_norm2 = lax.psum(
        product_nt(grad_gateup, gateup_w.reshape(gateup_w.shape[0], -1)).astype(jnp.bfloat16), "tp"
    ).astype(jnp.float32)
    _norm2_value, norm2_pull = jax.vjp(lambda values: rms_scale(values, norm2_gain), residual)
    grad_residual = cotangent.astype(jnp.float32) + norm2_pull(grad_norm2)[0]
    norm2_part = gain_part(residual, grad_norm2)
    grad_mix = grad_residual.astype(jnp.bfloat16)
    mamba_grad = product_tn(mamba_low, grad_mix)
    grad_mamba = product_nt(grad_mix, mamba_w)
    attn_grad = product_tn(attended_low, grad_mix)
    grad_attended = (
        product_nt(grad_mix, attn_w).reshape(row_count, heads_local, HD).astype(jnp.bfloat16)
    )

    def delta_step(block_idx, summed):
        scores, _keys, values_blk = block_scores(block_idx * KEY_BLOCK)
        probs = jnp.exp(scores - log_total[:, :, None])
        grad_probs = jnp.einsum(
            "qhd,kd->hqk", grad_attended, values_blk, preferred_element_type=jnp.float32
        )
        return summed + jnp.sum(probs * grad_probs, axis=-1)

    row_delta = lax.fori_loop(
        0, needed_blocks, delta_step, jnp.zeros((heads_local, row_count), jnp.float32)
    )

    def score_grads(block_start):
        scores, keys_blk, values_blk = block_scores(block_start)
        probs = jnp.exp(scores - log_total[:, :, None])
        grad_probs = jnp.einsum(
            "qhd,kd->hqk", grad_attended, values_blk, preferred_element_type=jnp.float32
        )
        grad_scores = (probs * (grad_probs - row_delta[:, :, None])).astype(jnp.bfloat16)
        return (grad_scores, probs, keys_blk)

    def query_step(block_idx, summed):
        grad_scores, _probs, keys_blk = score_grads(block_idx * KEY_BLOCK)
        return summed + jnp.einsum(
            "hqk,kd->qhd", grad_scores, keys_blk, preferred_element_type=jnp.float32
        )

    grad_qrot = lax.fori_loop(
        0, needed_blocks, query_step, jnp.zeros((row_count, heads_local, HD), jnp.float32)
    )
    grad_qrot = grad_qrot * score_scale
    q_all, attended_all, total_all, delta_all = (
        lax.all_gather(q_rot, "ctx", axis=0, tiled=True),
        lax.all_gather(grad_attended, "ctx", axis=0, tiled=True),
        lax.all_gather(log_total.astype(jnp.bfloat16), "ctx", axis=1, tiled=True).astype(
            log_total.dtype
        ),
        lax.all_gather(row_delta.astype(jnp.bfloat16), "ctx", axis=1, tiled=True).astype(
            row_delta.dtype
        ),
    )
    keys_mine = kv_local[:, :HD]
    values_mine = kv_local[:, HD:]

    def owner_step(block_idx, sums):
        grad_keys, grad_values = sums
        query_start = block_idx * KEY_BLOCK
        q_blk = lax.dynamic_slice_in_dim(q_all, query_start, KEY_BLOCK, 0)
        att_blk = lax.dynamic_slice_in_dim(attended_all, query_start, KEY_BLOCK, 0)
        total_blk = lax.dynamic_slice_in_dim(total_all, query_start, KEY_BLOCK, 1)
        delta_blk = lax.dynamic_slice_in_dim(delta_all, query_start, KEY_BLOCK, 1)
        qdocs_blk = lax.dynamic_slice_in_dim(key_docs, query_start, KEY_BLOCK, 0)
        qpos_blk = query_start + jnp.arange(KEY_BLOCK, dtype=jnp.int32)
        raw_scores = (
            jnp.einsum("qhd,kd->hqk", q_blk, keys_mine, preferred_element_type=jnp.float32)
            * score_scale
        )
        allowed = (qdocs_blk[:, None] == doc_ids[None, :]) & (
            positions[None, :] <= qpos_blk[:, None]
        )
        scores = jnp.where(allowed[None], raw_scores, MASKED)
        probs = jnp.exp(scores - total_blk[:, :, None])
        grad_probs = jnp.einsum(
            "qhd,kd->hqk", att_blk, values_mine, preferred_element_type=jnp.float32
        )
        grad_scores = (probs * (grad_probs - delta_blk[:, :, None])).astype(jnp.bfloat16)
        grad_keys = (
            grad_keys
            + jnp.einsum("hqk,qhd->kd", grad_scores, q_blk, preferred_element_type=jnp.float32)
            * score_scale
        )
        grad_values = grad_values + jnp.einsum(
            "hqk,qhd->kd", probs.astype(jnp.bfloat16), att_blk, preferred_element_type=jnp.float32
        )
        return (grad_keys, grad_values)

    start_sums = (jnp.zeros((row_count, HD), jnp.float32), jnp.zeros((row_count, HD), jnp.float32))
    owned_keys, owned_values = lax.fori_loop(
        first_row // KEY_BLOCK, key_blocks, owner_step, start_sums
    )
    grad_kv = jnp.concatenate([owned_keys, owned_values], axis=1)
    _rope_value, rope_pull = jax.vjp(lambda values: rope_turn(values, rel_pos), queries)
    grad_query = rope_pull(grad_qrot)[0].reshape(row_count, -1).astype(jnp.bfloat16)
    _key_value, key_pull = jax.vjp(lambda values: rope_turn(values, rel_pos), key_pre)
    grad_key = key_pull(grad_kv[:, None, :HD])[0][:, 0]
    grad_kv_mine = jnp.concatenate([grad_key, grad_kv[:, HD:]], axis=1).reshape(row_count, 2, HD)
    grad_keyval = lax.dynamic_update_slice_in_dim(
        jnp.zeros((row_count, 2, KVH * HD), jnp.float32), grad_kv_mine, kv_head * HD, 2
    )
    _finish_value, finish_pull = jax.vjp(
        finish, ssm_out, inner_vals, gate_z, skip_local, gain_local
    )
    grad_ssm, grad_inner_a, grad_gate, grad_skip, grad_gain = finish_pull(grad_mamba)
    _incoming_value, incoming_pull = jax.vjp(incoming, read_vec, log_decay, state_in)
    grad_read_a, grad_decay_a, grad_state_in = incoming_pull(grad_ssm)
    suffix = prefix_2((through, grad_state_in), "ctx", chain_step, identity_pair)
    grad_end = suffix[1]
    grad_through = jnp.sum(grad_end * state_in, axis=(1, 2))
    _local_value, local_pull = jax.vjp(
        local_states, inner_vals, step_size, log_decay, write_vec, read_vec
    )
    grad_inner_b, grad_step_b, grad_decay_b, grad_write, grad_read_b = local_pull(
        (grad_ssm, grad_end, grad_through)
    )
    _prepare_value, prepare_pull = jax.vjp(
        prepare, extended, step_raw, taps, bias_local, decay_local
    )
    grad_ext, grad_step_raw, grad_taps, grad_bias, grad_decay_log = prepare_pull(
        (
            grad_inner_a + grad_inner_b,
            grad_step_b,
            grad_decay_a + grad_decay_b,
            grad_write,
            grad_read_a + grad_read_b,
        )
    )
    edge_grad = passed_along(grad_ext[: CONV - 1], "ctx", -1)
    grad_body = grad_ext[CONV - 1 :]
    grad_mixed_in = jnp.concatenate(
        [grad_body[: row_count - (CONV - 1)], grad_body[row_count - (CONV - 1) :] + edge_grad],
        axis=0,
    )
    grad_inner = jnp.concatenate([grad_gate, grad_mixed_in[:, :inner_width]], axis=1).astype(
        jnp.bfloat16
    )
    grad_step = grad_step_raw.astype(jnp.bfloat16)
    inner_grad = product_tn(normed, grad_inner).reshape(inner_w.shape)
    step_grad = product_tn(normed, grad_step)
    query_grad = product_tn(normed, grad_query)
    grad_norm_part = (
        product_nt(grad_query, query_w)
        + product_nt(grad_inner, inner_w.reshape(inner_w.shape[0], -1))
        + product_nt(grad_step, step_w)
    )
    shared_part = jnp.concatenate(
        [grad_keyval.reshape(row_count, -1), grad_mixed_in[:, inner_width:]], axis=1
    )
    grad_norm_sum, shared_sum = (
        lax.psum(grad_norm_part.astype(jnp.bfloat16), "tp").astype(jnp.float32),
        lax.psum(shared_part.astype(jnp.bfloat16), "tp").astype(jnp.float32),
    )
    shared_low = shared_sum.astype(jnp.bfloat16)
    shared_w = jnp.concatenate(
        [keyval_w.reshape(keyval_w.shape[0], -1), state_w.reshape(state_w.shape[0], -1)], axis=1
    )
    grad_norm1 = grad_norm_sum + product_nt(shared_low, shared_w)
    shared_grad = product_tn(normed, shared_low)
    keyval_grad = shared_grad[:, : 2 * KVH * HD].reshape(keyval_w.shape)
    state_grad = shared_grad[:, 2 * KVH * HD :].reshape(state_w.shape)
    _norm1_value, norm1_pull = jax.vjp(lambda values: rms_scale(values, norm1_gain), hidden_in)
    tokens_grad = (grad_residual + norm1_pull(grad_norm1)[0]).astype(jnp.bfloat16)
    norm1_part = gain_part(hidden_in, grad_norm1)
    grads_out = (
        lax.psum_scatter(query_grad, ("dp", "ctx"), scatter_dimension=0, tiled=True),
        lax.psum_scatter(keyval_grad, ("dp", "ctx"), scatter_dimension=0, tiled=True),
        lax.psum_scatter(attn_grad, ("dp", "ctx"), scatter_dimension=1, tiled=True),
        lax.psum_scatter(inner_grad, ("dp", "ctx"), scatter_dimension=0, tiled=True),
        lax.psum_scatter(state_grad, ("dp", "ctx"), scatter_dimension=0, tiled=True),
        lax.psum_scatter(step_grad, ("dp", "ctx"), scatter_dimension=0, tiled=True),
        lax.psum_scatter(mamba_grad, ("dp", "ctx"), scatter_dimension=1, tiled=True),
        lax.psum_scatter(gateup_grad, ("dp", "ctx"), scatter_dimension=0, tiled=True),
        lax.psum_scatter(down_grad, ("dp", "ctx"), scatter_dimension=1, tiled=True),
    )

    def spread_out(values, full_shape, offset, axis_dim):
        return lax.dynamic_update_slice_in_dim(
            jnp.zeros(full_shape, jnp.float32), values, offset, axis_dim
        )

    small_out = lax.psum(
        (
            norm1_part,
            norm2_part,
            spread_out(grad_taps[:, :inner_width], conv_inner.shape, channel_start, 1),
            grad_taps[:, inner_width:].reshape(conv_state.shape),
            spread_out(grad_bias, step_bias.shape, head_start, 0),
            spread_out(grad_decay_log, decay_log.shape, head_start, 0),
            spread_out(grad_skip, skip_gain.shape, head_start, 0),
            spread_out(grad_gain, mamba_gain.shape, channel_start, 0),
        ),
        ("dp", "ctx", "tp"),
    )
    return (
        layer_out,
        tokens_grad,
        small_out[0],
        small_out[1],
        grads_out[0],
        grads_out[1],
        grads_out[2],
        grads_out[3],
        grads_out[4],
        grads_out[5],
        small_out[2],
        small_out[3],
        small_out[4],
        small_out[5],
        small_out[6],
        small_out[7],
        grads_out[6],
        grads_out[7],
        grads_out[8],
    )


def solution(mesh):
    return jax.shard_map(
        body,
        mesh=mesh,
        in_specs=(
            P(("dp", "ctx"), None),
            P(("dp", "ctx"), None),
            P("dp", None),
            P(),
            P(),
            P(("dp", "ctx"), "tp"),
            P(("dp", "ctx"), None, None),
            P("tp", ("dp", "ctx")),
            P(("dp", "ctx"), None, "tp"),
            P(("dp", "ctx"), None, None),
            P(("dp", "ctx"), "tp"),
            P(),
            P(),
            P(),
            P(),
            P(),
            P(),
            P("tp", ("dp", "ctx")),
            P(("dp", "ctx"), None, "tp"),
            P("tp", ("dp", "ctx")),
        ),
        out_specs=(
            P(("dp", "ctx"), None),
            P(("dp", "ctx"), None),
            P(),
            P(),
            P(("dp", "ctx"), "tp"),
            P(("dp", "ctx"), None, None),
            P("tp", ("dp", "ctx")),
            P(("dp", "ctx"), None, "tp"),
            P(("dp", "ctx"), None, None),
            P(("dp", "ctx"), "tp"),
            P(),
            P(),
            P(),
            P(),
            P(),
            P(),
            P("tp", ("dp", "ctx")),
            P(("dp", "ctx"), None, "tp"),
            P("tp", ("dp", "ctx")),
        ),
        check_vma=False,
    )
```

profile of v0, /device:TPU:0, one launch (start us, length us, event | category | flops | bytes accessed | tf_op | source)
XLA Modules:
  0.0 1714.0 jit_solution(8330554599167716963)
XLA Ops:
  14.6 31.0 %all_gather.69 = bf16[1024,2,128]{0,2,1:T(8,128)(2,1)S(1)} all-gather(bf16[128,2,128]{0,2,1:T(8,128)(2,1)S(1)} %copy.351), channel_id=1, replica_groups=mesh['dp'=4,'ctx'=2,'tp'=4] {'dp','ctx'}, dimensions={0}, use_global_device_ids=true | all-gather | bytes 589824 | tf_op jit(solution)/shard_map/all_gather | solution.py:212
  50.3 31.7 %all_gather.75 = bf16[1024,2,128]{2,1,0:T(2,128)(2,1)S(1)} all-gather(bf16[128,2,128]{2,1,0:T(2,128)(2,1)S(1)} %copy-done.112), channel_id=1, replica_groups=mesh['dp'=4,'ctx'=2,'tp'=4] {'dp','ctx'}, dimensions={0}, use_global_device_ids=true | all-gather | bytes 589824 | tf_op jit(solution)/shard_map/all_gather | solution.py:215
  83.8 26.4 %all_gather.73 = bf16[1024,6]{0,1:T(8,128)(2,1)S(1)} all-gather(bf16[128,6]{0,1:T(8,128)(2,1)S(1)} %copy-done.155), channel_id=1, replica_groups=mesh['dp'=4,'ctx'=2,'tp'=4] {'dp','ctx'}, dimensions={0}, use_global_device_ids=true | all-gather | bytes 13824 | tf_op jit(solution)/shard_map/all_gather | solution.py:216
  135.5 31.0 %all_gather.71 = bf16[1024,128]{1,0:T(8,128)(2,1)S(1)} all-gather(bf16[128,128]{1,0:T(8,128)(2,1)} %param.45), channel_id=1, replica_groups=mesh['dp'=4,'ctx'=2,'tp'=4] {'dp','ctx'}, dimensions={0}, use_global_device_ids=true | all-gather | bytes 294912 | tf_op jit(solution)/shard_map/all_gather | solution.py:211
  184.6 36.4 %all_gather.72 = bf16[128,1024]{1,0:T(8,128)(2,1)S(1)} all-gather(bf16[128,128]{1,0:T(8,128)(2,1)S(1)} %copy-done.134), channel_id=1, replica_groups=mesh['dp'=4,'ctx'=2,'tp'=4] {'dp','ctx'}, dimensions={1}, use_global_device_ids=true | all-gather | bytes 294912 | tf_op jit(solution)/shard_map/all_gather | solution.py:213
  221.0 29.1 %all_gather.79 = bf16[384,1024]{1,0:T(8,128)(2,1)} all-gather(bf16[384,128]{1,0:T(8,128)(2,1)} %param.57), channel_id=1, replica_groups=mesh['dp'=4,'ctx'=2,'tp'=4] {'dp','ctx'}, dimensions={1}, use_global_device_ids=true | all-gather | bytes 884736 | tf_op jit(solution)/shard_map/all_gather | solution.py:217
  279.9 98.7 %while.151 = (s32[]{:T(128)}, f32[6,64,128]{2,1,0:T(8,128)}, s32[]{:T(128)}, f32[4,256,6,64]{1,0,3,2:T(4,128)}, s32[4,256]{1,0:T(4,128)S(1)}, /*index=5*/f32[4,2...) while((s32[]{:T(128)}, f32[6,64,128]{2,1,0:T(8,128)}, ...), condition=%wide.region_14.15_spmd.clone, body=%wide.region_11.14_spmd.clone.sunk | while | flops 707107584 | bytes 5448082 | solution.py:178
  417.9 34.0 %all-reduce.33.cloned.1.call-done = bf16[1024,1024]{1,0:T(8,128)(2,1)} async-done(((bf16[1024,1024]{1,0:T(8,128)(2,1)}), bf16[1024,1024]{1,0:T(8,128)(2,1)}) %all-reduce.33.cloned.1.call-update) | async-done | bytes 2097168 | tf_op jit(solution)/shard_map/psum | solution.py:359
  461.5 32.2 %all-gather.11.cloned.1.call-done = bf16[512,1024]{1,0:T(8,128)(2,1)} async-done(((bf16[512,128]{1,0:T(8,128)(2,1)}), bf16[512,1024]{1,0:T(8,128)(2,1)}) %all-gather.11.cloned.1.call-update) | async-done | bytes 1048592 | tf_op jit(solution)/shard_map/all_gather | solution.py:219
  506.0 36.8 %while.153 = (s32[]{:T(128)}, f32[6,64,128]{2,1,0:T(8,128)S(1)}, s32[]{:T(128)}, f32[4,6,64,128]{3,2,1,0:T(8,128)}, s32[4]{0:T(128)S(1)}, /*index=5*/s32[4,256]{...) while((s32[]{:T(128)}, f32[6,64,128]{2,1,0:T(8,128)S(1)}, ...), condition=%wide.region_38.39_spmd.clone, body=%wide.region_35.38_spmd.clone.sunk | while | flops 151491360 | bytes 1413014 | solution.py:178
  588.1 212.6 %while.145 = (s32[]{:T(128)}, f32[6,64,128]{2,1,0:T(8,128)}, f32[4,256,6,64]{1,0,3,2:T(4,128)}, f32[4,256,6]{1,2,0:T(8,128)}, f32[4,256,6]{1,2,0:T(8,128)}, /*in...) while((s32[]{:T(128)}, f32[6,64,128]{2,1,0:T(8,128)}, ...), condition=%wide.region_51.52_spmd, body=%wide.region_39.51_spmd.sunk | while | flops 1669331712 | bytes 22442004 | solution.py:178
  830.8 13.2 all_gather.86
  844.0 16.1 while.148
  860.1 17.9 %all_gather.87 = bf16[2,2048]{1,0:T(2,128)(2,1)S(1)} all-gather(bf16[2,1024]{1,0:T(2,128)(2,1)S(1)} %convert_element_type.304), channel_id=1, replica_groups=mesh['dp'=4,'ctx'=2,'tp'=4] {'ctx'}, dimensions={1}, use_global_device_ids=true | all-gather | bytes 12288 | tf_op jit(solution)/shard_map/all_gather | solution.py:447
  879.5 44.5 %while.150 = (s32[]{:T(128)}, f32[1024,64]{0,1:T(8,128)}, f32[1024,64]{0,1:T(8,128)}, s32[2048]{0:T(1024)S(1)}, s32[1024]{0:T(1024)S(1)}, /*index=5*/bf16[2048,2...) while((s32[]{:T(128)}, f32[1024,64]{0,1:T(8,128)}, ...), condition=%wide.region_58.59_spmd.clone, body=%wide.region_57.58_spmd.clone.sunk | while | flops 549127680 | bytes 34917676 | solution.py:487
  935.6 18.5 %while.149 = (s32[]{:T(128)}, f32[1024,2,64]{0,2,1:T(8,128)}, s32[]{:T(128)}, bf16[2048,128]{0,1:T(8,128)(2,1)}, s32[1024]{0:T(1024)S(1)}, /*index=5*/s32[2048]{...) while((s32[]{:T(128)}, f32[1024,2,64]{0,2,1:T(8,128)}, ...), condition=%wide.region_31.32_spmd.clone, body=%wide.region_30.31_spmd.clone.sunk | while | flops 410650112 | bytes 11280123 | solution.py:437
  995.6 75.0 %all-reduce.39.cloned.1.call-done = (bf16[1024,1024]{1,0:T(8,128)(2,1)}, bf16[1024,1024]{1,0:T(8,128)(2,1)}, bf16[1024,512]{0,1:T(8,128)(2,1)}) async-done(((bf16[1024,1024]{1,0:T(8,128)(2,1)}, bf16[1024,1024]{1,0:T(8,128)(2,1)}, bf16[1024,512]{0,1:T(8,128)(2,1)}), (bf16[1024,1024]{1,0:T(8,128)(2,1)}, bf16[1024,1024]{1,0:T(8,128)(2,1)}, bf16[1024,512]{0,1:T(8,128)(2,1)})) %all-reduce.39.cloned.1.call-update) | async-done | bytes 5242896 | tf_op jit(solution)/shard_map/psum | solution.py:368
  1115.5 44.5 %all-reduce.25 = (f32[1024]{0:T(1024)}, f32[1024]{0:T(1024)}, f32[5,1536]{1,0:T(8,128)}, f32[5,2,128]{2,1,0:T(2,128)}, f32[24]{0:T(128)}, /*index=5*/f32[24]{0:T(128)}, f32[24]{0:T(128)}, f32[1536]{0:T(1024)}) all-reduce(f32[1024]{0:T(1024)S(1)} %multiply_reduce_fusion.16, ...), channel_id=1, replica_groups=mesh['dp'=4,'ctx'=2,'tp'=4] {'dp','ctx','tp'}, use_global_device_ids=true, to_apply=%region_63.64 | all-reduce | flops 12616 | bytes 100928 | tf_op jit(solution)/shard_map/psum | solution.py:579
  1167.8 212.2 %all-reduce.37.cloned.1.call-done = (f32[1024,2,128]{2,1,0:T(2,128)}, f32[1024,2,384]{2,1,0:T(2,128)}, f32[1024,2,128]{2,1,0:T(2,128)}, f32[1024,2,512]{2,1,0:T(2,128)}) async-done(((f32[1024,2,128]{2,1,0:T(2,128)}, f32[1024,2,384]{2,1,0:T(2,128)}, f32[1024,2,128]{2,1,0:T(2,128)}, f32[1024,2,512]{2,1,0:T(2,128)}), (f32[1024,2,128]{2,1,0:T(2,128)}, f32[1024,2,384]{2,1,0:T(2,128)}, f32[1024,2,128]{2,1,0:T(2,128)}, ...) | async-done | bytes 9437200
  1385.4 50.9 %reduce-scatter.10.cloned.1.call-done = f32[128,6]{0,1:T(8,128)} async-done(((f32[1024,6]{0,1:T(8,128)}), f32[128,6]{0,1:T(8,128)}) %reduce-scatter.10.cloned.1.call-update) | async-done | bytes 3088 | tf_op jit(solution)/shard_map/reduce_scatter | solution.py:568
  1436.2 65.4 %reduce-scatter.8.cloned.1.call-done = f32[128,128]{1,0:T(8,128)} async-done(((f32[128,1024]{1,0:T(8,128)}), f32[128,128]{1,0:T(8,128)}) %reduce-scatter.8.cloned.1.call-update) | async-done | bytes 65552 | tf_op jit(solution)/shard_map/reduce_scatter | solution.py:565
  1501.6 65.1 %reduce-scatter.6.cloned.1.call-done = f32[128,128]{1,0:T(8,128)} async-done(((f32[1024,128]{1,0:T(8,128)}), f32[128,128]{1,0:T(8,128)}) %reduce-scatter.6.cloned.1.call-update) | async-done | bytes 65552 | tf_op jit(solution)/shard_map/reduce_scatter | solution.py:563
  1566.7 68.7 %reduce-scatter.12.cloned.1.call-done = f32[384,128]{1,0:T(8,128)} async-done(((f32[384,1024]{1,0:T(8,128)}), f32[384,128]{1,0:T(8,128)}) %reduce-scatter.12.cloned.1.call-update) | async-done | bytes 196624 | tf_op jit(solution)/shard_map/reduce_scatter | solution.py:569
  1635.4 71.5 %reduce-scatter.14.cloned.1.call-done = f32[512,128]{1,0:T(8,128)} async-done(((f32[512,1024]{1,0:T(8,128)}), f32[512,128]{1,0:T(8,128)}) %reduce-scatter.14.cloned.1.call-update) | async-done | bytes 262160 | tf_op jit(solution)/shard_map/reduce_scatter | solution.py:571
  (1158 shorter events, 754.1 us)
Async XLA Ops:
  7.2 117.0 %copy-start = (f32[5,1536]{1,0:T(8,128)S(1)}, f32[5,1536]{1,0:T(8,128)}, u32[]{:S(2)}) copy-start(f32[5,1536]{1,0:T(8,128)} %param.51) | copy-start | bytes 92164
  7.2 246.4 %all-gather.7.cloned.1.call-start = ((), (), s32[]{:S(2)}) async-start(), calls=%async_computation.5 | async-start | bytes 1769472 | tf_op jit(solution)/shard_map/all_gather | solution.py:214
  8.0 406.4 %all-gather.9.cloned.1.call-start = ((), (), s32[]{:S(2)}) async-start(), calls=%async_computation.7 | async-start | bytes 2359296 | tf_op jit(solution)/shard_map/all_gather | solution.py:218
  8.7 443.2 %all-reduce.33.cloned.1.call-start = ((), (), s32[]{:S(2)}) async-start(), calls=%async_computation.6 | async-start | bytes 4194304 | tf_op jit(solution)/shard_map/psum | solution.py:359
  12.3 114.5 %copy-start.109 = (f32[1024]{0:T(1024)}, f32[1024]{0:T(1024)S(1)}, u32[]{:S(2)}) copy-start(f32[1024]{0:T(1024)S(1)} %fusion.244) | copy-start | bytes 12292
  12.3 114.5 %copy-start.150 = (f32[32]{0:T(128)}, f32[32]{0:T(128)S(1)}, u32[]{:S(2)}) copy-start(f32[32]{0:T(128)S(1)} %multiply_power_fusion) | copy-start | bytes 388
  50.2 77.3 %copy-start.81 = (bf16[1024,64]{0,1:T(8,128)(2,1)}, bf16[1024,64]{0,1:T(8,128)(2,1)S(1)}, u32[]{:S(2)}) copy-start(bf16[1024,64]{0,1:T(8,128)(2,1)S(1)} %slice.374) | copy-start | bytes 393220
  123.6 126.6 %copy-start.88 = (f32[1,6,8,128]{3,2,1,0:T(8,128)}, f32[1,6,8,128]{3,2,1,0:T(8,128)S(1)}, u32[]{:S(2)}) copy-start(f32[1,6,8,128]{3,2,1,0:T(8,128)S(1)} %exponential_bitcast_fusion) | copy-start | bytes 73732
  175.3 74.9 %copy-start.135 = (f32[1,5,2,128]{3,1,2,0:T(8,128)S(1)}, f32[1,5,2,128]{3,1,2,0:T(8,128)}, u32[]{:S(2)}) copy-start(f32[1,5,2,128]{3,1,2,0:T(8,128)} %copy.501) | copy-start | bytes 15364
  175.3 74.9 %copy-start.130 = (f32[1024]{0:T(1024)S(1)}, f32[1024]{0:T(1024)}, u32[]{:S(2)}) copy-start(f32[1024]{0:T(1024)} %compare_convert_fusion.2) | copy-start | bytes 12292
  183.2 70.4 %copy-start.82 = (s32[2048]{0:T(1024)}, s32[2048]{0:T(1024)S(1)}, u32[]{:S(2)}) copy-start(s32[2048]{0:T(1024)S(1)} %get-tuple-element.2934) | copy-start | bytes 24580
  257.5 4.6 collective-permute-start
  400.5 93.1 %all-gather.11.cloned.1.call-start = ((), (), s32[]{:S(2)}) async-start(), calls=%async_computation.8 | async-start | bytes 1179648 | tf_op jit(solution)/shard_map/all_gather | solution.py:219
  401.1 155.2 %all-reduce.35.cloned.1.call-start = ((), (), s32[]{:S(2)}) async-start(), calls=%async_computation.9 | async-start | bytes 4194304 | tf_op jit(solution)/shard_map/psum | solution.py:396
  457.1 103.2 %copy-start.126 = (f32[1024]{0:T(1024)}, f32[1024]{0:T(1024)S(1)}, u32[]{:S(2)}) copy-start(f32[1024]{0:T(1024)S(1)} %fusion.241) | copy-start | bytes 12292
  505.8 564.8 %all-reduce.39.cloned.1.call-start = ((), (), s32[]{:S(2)}) async-start(), calls=%async_computation.16 | async-start | bytes 10485760 | tf_op jit(solution)/shard_map/psum | solution.py:368
  827.9 131.6 %collective-permute-start.1 = (f32[3,640]{0,1:T(8,128)}, f32[3,640]{0,1:T(8,128)}, u32[]{:S(2)}, u32[]{:S(2)}) collective-permute-start(f32[3,640]{0,1:T(8,128)} %pad_add_fusion.1), channel_id=1, source_target_pairs={{4,0},{5,1},{6,2},{7,3},{12,8},{13,9},{14,10},{15,11},{20,16},{21,... | collective-permute-start | bytes 23048 | tf_op jit(solution)/shard_map/ppermute | solution.py:24
  968.3 411.7 %all-reduce.37.cloned.1.call-start = ((), (), s32[]{:S(2)}) async-start(), calls=%async_computation.15 | async-start | bytes 18874368
  1078.6 357.7 %reduce-scatter.10.cloned.1.call-start = ((), (), s32[]{:S(2)}) async-start(), calls=%async_computation.12 | async-start | bytes 36864 | tf_op jit(solution)/shard_map/reduce_scatter | solution.py:568
  1081.2 420.4 %reduce-scatter.8.cloned.1.call-start = ((), (), s32[]{:S(2)}) async-start(), calls=%async_computation.11 | async-start | bytes 589824 | tf_op jit(solution)/shard_map/reduce_scatter | solution.py:565
  1084.2 482.5 %reduce-scatter.6.cloned.1.call-start = ((), (), s32[]{:S(2)}) async-start(), calls=%async_computation.10 | async-start | bytes 589824 | tf_op jit(solution)/shard_map/reduce_scatter | solution.py:563
  1087.8 547.6 %reduce-scatter.12.cloned.1.call-start = ((), (), s32[]{:S(2)}) async-start(), calls=%async_computation.13 | async-start | bytes 1769472 | tf_op jit(solution)/shard_map/reduce_scatter | solution.py:569
  1091.6 615.3 %reduce-scatter.14.cloned.1.call-start = ((), (), s32[]{:S(2)}) async-start(), calls=%async_computation.14 | async-start | bytes 2359296 | tf_op jit(solution)/shard_map/reduce_scatter | solution.py:571
  1160.1 546.8 %copy-start.1 = (f32[5,1536]{1,0:T(8,128)S(1)}, f32[5,1536]{1,0:T(8,128)}, u32[]{:S(2)}) copy-start(f32[5,1536]{1,0:T(8,128)} %param.51) | copy-start | bytes 92164
  (224 other events, 2412.4 us)
Sparse Core Ops, SparseCore 0:
  10.3 51.4 all-gather.6
  63.9 49.1 all-gather.8
  400.6 51.2 all-reduce.32
  454.0 39.5 all-gather.10
  505.9 50.3 all-reduce.34
  968.4 102.2 all-reduce.38
  1078.7 301.2 all-reduce.36
  1383.7 52.4 reduce-scatter.9
  1440.2 61.3 reduce-scatter.7
  1505.7 60.9 reduce-scatter.5
  1570.7 64.6 reduce-scatter.11
  1639.8 67.0 reduce-scatter.13
where the time goes:
time: 1730 us; the launch traced here: 1710 us
  waiting for transfers between devices  687 us (40%)
  blocking collectives  297 us (17%)
  matrix products  269 us (16%)
  local copies, waits for them, and re-layouts  225 us (13%)
  other arithmetic  193 us (11%)
  between operations  19 us (1%)
  loops' own time  18.8 us (1%)
    unnamed x13, waiting for transfers between devices  214 us
    dynamic_update_slice x24, local copies, waits for them, and re-layouts, state_scan(): lax.scan(jax.checkpoint(scan_block), (start_state, jnp.array(-1, jnp.int3...  85.3 us
    psum x1, waiting for transfers between devices, body(): lax.psum(product(hidden_act, down_w).astype(jnp.bfloat16), 'tp')  75 us
    reduce_scatter x1, waiting for transfers between devices, body(): lax.psum_scatter(down_grad, ('dp', 'ctx'), scatter_dimension=1, tiled=True)  71.5 us
    another operation x50, other arithmetic  69.4 us
    reduce_scatter x1, waiting for transfers between devices, body(): lax.psum_scatter(mamba_grad, ('dp', 'ctx'), scatter_dimension=1, tiled=True)  68.7 us
    reduce_scatter x1, waiting for transfers between devices, body(): lax.psum_scatter(attn_grad, ('dp', 'ctx'), scatter_dimension=1, tiled=True)  65.4 us
    reduce_scatter x1, waiting for transfers between devices, body(): lax.psum_scatter(query_grad, ('dp', 'ctx'), scatter_dimension=0, tiled=True)  65.1 us
  transfers between devices with their start and end apart: 14, of which 11 were waited for; matrix products, arithmetic and copies ran while one was open for 23% of the time, Pallas kernels for 0%

commit v1 on v0

v1 whole, which is shorter than its diff:
```python
import functools

import jax
import jax.numpy as jnp
from jax import lax
from jax.experimental import pallas as pl
from jax.experimental.pallas import tpu as pltpu
from jax.sharding import PartitionSpec as P

H = 8
KVH = 2
HD = 64
PD = 64
NST = 128
CONV = 4
CHUNK = 256
QUERY_BLOCK = 256
KEY_BLOCK = 512
EDGE = 8
LANES = 128
VMEM_BYTES = 48 * 1024 * 1024

EPS = 1e-05
ROPE_BASE = 10000.0
MASKED = -1e30
HIGH = lax.Precision.HIGHEST
F32 = jnp.float32
BF16 = jnp.bfloat16
WEIGHT_AXES = ("dp", "ctx")


def product(left, right):
    return jnp.dot(left, right, preferred_element_type=F32)


def product_tn(left, right):
    return lax.dot_general(left, right, (((0,), (0,)), ((), ())), preferred_element_type=F32)


def product_nt(left, right):
    return lax.dot_general(left, right, (((1,), (1,)), ((), ())), preferred_element_type=F32)


def low_nn(left, right):
    return product(left.astype(BF16), right.astype(BF16))


def low_tn(left, right):
    return product_tn(left.astype(BF16), right.astype(BF16))


def low_nt(left, right):
    return product_nt(left.astype(BF16), right.astype(BF16))


def split_nn(left, ones):
    first = left.astype(BF16)
    second = (left - first.astype(F32)).astype(BF16)
    return product(first, ones) + product(second, ones)


def split_nt(ones, right):
    first = right.astype(BF16)
    second = (right - first.astype(F32)).astype(BF16)
    return product_nt(ones, first) + product_nt(ones, second)


def iota(shape, dim):
    return lax.broadcasted_iota(jnp.int32, shape, dim)


def start_of(rows, meta, docs):
    start = jnp.full(rows.shape, meta[0], jnp.int32)
    for doc in range(1, docs):
        start = jnp.where(rows >= meta[doc], meta[doc], start)
    return start


def start_of_one(row, meta, docs):
    start = meta[0]
    for doc in range(1, docs):
        start = jnp.where(row >= meta[doc], meta[doc], start)
    return start


def sigmoid(values):
    return 1.0 / (1.0 + jnp.exp(-values))


def swap_halves(values):
    lane = iota(values.shape, 1)
    up = pltpu.roll(values, LANES - HD // 2, 1)
    down = pltpu.roll(values, HD // 2, 1)
    return jnp.where(lane % HD < HD // 2, up, down)


def prep_kernel(
    docs,
    inner_width,
    meta,
    proj,
    edge,
    taps,
    heads,
    cosine,
    sine,
    spread,
    spread_t,
    q_out,
    kv_out,
    mixed_out,
    act_out,
    slope_out,
    step_out,
    sig_out,
    cum_out,
    state_out,
    end_out,
    ext,
    state,
    total_log,
):
    c = pl.program_id(0)
    rows = proj.shape[0]
    mix = ext.shape[1]
    row = c * rows + iota((rows, 1), 0)
    rel = row - start_of(row, meta, docs)
    mixed = proj[:, inner_width : inner_width + mix].astype(BF16)
    mixed_out[...] = mixed

    @pl.when(c == 0)
    def _():
        ext[0:EDGE] = edge[...]
        state[...] = jnp.zeros_like(state)
        total_log[...] = jnp.zeros_like(total_log)

    @pl.when(c > 0)
    def _():
        ext[0:EDGE] = ext[rows : rows + EDGE]

    ext[EDGE : EDGE + rows] = mixed.astype(F32)
    pre = jnp.broadcast_to(taps[CONV : CONV + 1, :], (rows, mix))
    for lag in range(CONV):
        keep = (rel >= lag).astype(F32)
        pre = pre + taps[CONV - 1 - lag : CONV - lag, :] * (
            ext[EDGE - lag : EDGE - lag + rows] * keep
        )
    sig = sigmoid(pre)
    act = pre * sig
    act_out[...] = act
    slope_out[...] = sig * (1.0 + pre * (1.0 - sig))

    base = inner_width + mix
    cos, sin = (cosine[...], sine[...])
    queries = proj[:, base : base + LANES]
    turned = queries * cos + swap_halves(queries) * sin
    q_out[...] = (turned * HD ** (-0.5)).astype(BF16)
    keyval = proj[:, base + LANES : base + 2 * LANES]
    is_key = iota(keyval.shape, 1) < HD
    kv_out[...] = jnp.where(is_key, keyval * cos + swap_halves(keyval) * sin, keyval).astype(BF16)

    raw = proj[:, base + 2 * LANES : base + 3 * LANES] + heads[0:1, :]
    step = jnp.maximum(raw, 0.0) + jnp.log1p(jnp.exp(-jnp.abs(raw)))
    decay = -step * heads[1:2, :]
    lower = (iota((rows, rows), 0) >= iota((rows, rows), 1)).astype(F32)
    cum = jnp.dot(lower, decay, precision=HIGH, preferred_element_type=F32)
    step_out[...] = step
    sig_out[...] = sigmoid(raw)
    cum_out[...] = cum

    last = c * rows + rows - 1
    last_start = start_of_one(last, meta, docs)
    total = cum[rows - 1 : rows, :]
    tail = jnp.where(row >= last_start, jnp.exp(total - cum), 0.0) * step
    goes_on = jnp.where(last_start < c * rows, 1.0, 0.0)
    kept = split_nt(spread_t[...], jnp.broadcast_to(jnp.exp(total) * goes_on, (NST, LANES)))
    state_out[...] = state[...]
    added = low_tn(act[:, :inner_width] * split_nn(tail, spread[...]), act[:, inner_width : inner_width + NST])
    state[...] = kept * state[...] + added
    total_log[...] = total_log[...] + jnp.broadcast_to(total, total_log.shape)

    @pl.when(c == pl.num_programs(0) - 1)
    def _():
        through = jnp.exp(total_log[0:1, :]) * jnp.where(last_start < 0, 1.0, 0.0)
        first = through.astype(BF16)
        second = (through - first.astype(F32)).astype(BF16)
        sub = iota((16, LANES), 0)
        end_out[0:inner_width] = state[...].astype(BF16)
        end_out[inner_width : inner_width + 16] = jnp.where(
            sub == 0, first.astype(F32), jnp.where(sub == 1, second.astype(F32), 0.0)
        ).astype(BF16)


def intra_kernel(docs, inner_width, meta, act, step, cum, spread, y_out):
    c = pl.program_id(0)
    rows = act.shape[0]
    row = iota((rows, 1), 0)
    first = start_of(c * rows + row, meta, docs) - c * rows
    col = iota((rows, rows), 1)
    linked = (col >= first) & (col <= iota((rows, rows), 0))
    couple = low_nt(act[:, inner_width + NST :], act[:, inner_width : inner_width + NST])
    weighted = (act[:, :inner_width] * split_nn(step[...], spread[...])).astype(BF16)
    cum_now = cum[...]
    cum_t = cum_now.T
    lane = iota((rows, LANES), 1)
    for pair in range(inner_width // LANES):
        values = weighted[:, pair * LANES : (pair + 1) * LANES]
        results = []
        for head in (2 * pair, 2 * pair + 1):
            arg = cum_now[:, head : head + 1] - cum_t[head : head + 1, :]
            mixing = couple * jnp.exp(jnp.where(linked, arg, MASKED))
            results.append(product(mixing.astype(BF16), values))
        y_out[:, pair * LANES : (pair + 1) * LANES] = jnp.where(lane < PD, results[0], results[1])


def two_heads(values, upper):
    values = values.astype(F32)
    lane = iota(values.shape, 1)
    rolled = pltpu.roll(values, HD, 1)
    keep = lane >= HD if upper else lane < HD
    pair = (rolled, values) if upper else (values, rolled)
    return jnp.concatenate([jnp.where(keep, part, 0.0) for part in pair], axis=0)


def attend_kernel(docs, meta, q, kv, out, lse_out):
    block = pl.program_id(0)
    rows = q.shape[0]
    first_row = meta[docs]
    row = block * rows + iota((rows, 1), 0)
    start = start_of(row, meta, docs)
    queries = two_heads(q[...], False).astype(BF16)
    low_block = (start_of_one(block * rows, meta, docs) + first_row) // KEY_BLOCK
    high_block = (first_row + (block + 1) * rows + KEY_BLOCK - 1) // KEY_BLOCK

    def one(index, sums):
        top, total, summed = sums
        at = pl.multiple_of(index * KEY_BLOCK, KEY_BLOCK)
        keyval = kv[pl.ds(at, KEY_BLOCK), :]
        scores = product_nt(queries, keyval)
        key = index * KEY_BLOCK - first_row + iota((rows, KEY_BLOCK), 1)
        allowed = (key >= start) & (key <= row)
        allowed = jnp.concatenate([allowed, allowed], axis=0)
        scores = jnp.where(allowed, scores, MASKED)
        new_top = jnp.maximum(top, jnp.max(scores, axis=1, keepdims=True))
        scale = jnp.exp(top - new_top)
        probs = jnp.exp(scores - new_top)
        total = total * scale + jnp.sum(probs, axis=1, keepdims=True)
        return (new_top, total, summed * scale + product(probs.astype(BF16), keyval))

    top, total, summed = lax.fori_loop(
        low_block,
        high_block,
        one,
        (
            jnp.full((2 * rows, 1), MASKED, F32),
            jnp.zeros((2 * rows, 1), F32),
            jnp.zeros((2 * rows, LANES), F32),
        ),
    )
    result = summed / total
    lse = top + jnp.log(total)
    lane = iota((rows, LANES), 1)
    out[...] = jnp.where(lane < HD, pltpu.roll(result[:rows], HD, 1), result[rows:]).astype(BF16)
    lse_out[...] = jnp.where(lane < HD, lse[:rows], lse[rows:])


def attend_back_kernel(docs, meta, q, kv, grad, att, lse, cosine, sine, gq_out, gkv_out):
    block = pl.program_id(0)
    rows = q.shape[0]
    first_row = meta[docs]

    @pl.when(block == 0)
    def _():
        gkv_out[...] = jnp.zeros_like(gkv_out)

    row = block * rows + iota((rows, 1), 0)
    start = start_of(row, meta, docs)
    queries = two_heads(q[...], False).astype(BF16)
    grads = two_heads(grad[...].astype(BF16), True)
    lse_now = lse[...]
    lse_col = jnp.concatenate([lse_now[:, 0:1], lse_now[:, HD : HD + 1]], axis=0)
    delta = jnp.sum(grads * two_heads(att[...], True), axis=1, keepdims=True)
    grads = grads.astype(BF16)
    low_block = (start_of_one(block * rows, meta, docs) + first_row) // KEY_BLOCK
    high_block = (first_row + (block + 1) * rows + KEY_BLOCK - 1) // KEY_BLOCK

    def one(index, summed):
        at = pl.multiple_of(index * KEY_BLOCK, KEY_BLOCK)
        keyval = kv[pl.ds(at, KEY_BLOCK), :]
        scores = product_nt(queries, keyval)
        key = index * KEY_BLOCK - first_row + iota((rows, KEY_BLOCK), 1)
        allowed = (key >= start) & (key <= row)
        allowed = jnp.concatenate([allowed, allowed], axis=0)
        probs = jnp.exp(jnp.where(allowed, scores - lse_col, MASKED))
        grad_scores = (probs * (product_nt(grads, keyval) - delta)).astype(BF16)
        gkv_out[pl.ds(at, KEY_BLOCK), :] += product_tn(grad_scores, queries) + product_tn(
            probs.astype(BF16), grads
        )
        return summed + product(grad_scores, keyval)

    summed = lax.fori_loop(low_block, high_block, one, jnp.zeros((2 * rows, LANES), F32))
    lane = iota((rows, LANES), 1)
    grad_q = jnp.where(lane < HD, summed[:rows], pltpu.roll(summed[rows:], HD, 1)) * HD ** (-0.5)
    gq_out[...] = (grad_q * cosine[...] - swap_halves(grad_q) * sine[...]).astype(BF16)


def finish_kernel(
    docs,
    inner_width,
    meta,
    y_in,
    act,
    cum,
    gate,
    att,
    state_local,
    state_in,
    params,
    spread,
    spread_t,
    block_ones,
    low_out,
    y_out,
    state_out,
    carry,
):
    c = pl.program_id(0)
    rows = act.shape[0]

    @pl.when(c == 0)
    def _():
        carry[...] = state_in[...]

    row = c * rows + iota((rows, 1), 0)
    start = start_of(row, meta, docs)
    last_start = start_of_one(c * rows + rows - 1, meta, docs)
    cum_now = cum[...]
    inflow = jnp.where(start < c * rows, jnp.exp(cum_now), 0.0)
    state = state_local[...] + carry[...]
    state_out[...] = state
    inner = act[:, :inner_width]
    y = y_in[...] + low_nt(act[:, inner_width + NST :], state) * split_nn(inflow, spread[...])
    y_out[...] = y
    total = jnp.exp(cum_now[rows - 1 : rows, :]) * jnp.where(last_start < c * rows, 1.0, 0.0)
    carry[...] = carry[...] * split_nt(spread_t[...], jnp.broadcast_to(total, (NST, LANES)))
    gate_now = gate[...]
    gated = (y + params[0:1, :] * inner) * (gate_now * sigmoid(gate_now))
    mean = split_nn(gated * gated, block_ones[...]) * (1.0 / PD)
    low = gated * lax.rsqrt(mean + EPS) * params[1:2, :]
    low_out[:, :LANES] = att[...]
    low_out[:, LANES:] = low.astype(BF16)


def finish_back_kernel(
    docs,
    inner_width,
    meta,
    grad,
    y_in,
    act,
    cum,
    gate,
    params,
    spread,
    block_ones,
    gy_out,
    gate_out,
    params_out,
    state_out,
    so_far,
):
    c = pl.program_id(0)
    rows = act.shape[0]

    @pl.when(c == 0)
    def _():
        params_out[...] = jnp.zeros_like(params_out)
        state_out[...] = jnp.zeros_like(state_out)
        so_far[...] = jnp.zeros_like(so_far)

    row = c * rows + iota((rows, 1), 0)
    start = start_of(row, meta, docs)
    cum_now = cum[...]
    inner = act[:, :inner_width]
    skip, gain = (params[0:1, :], params[1:2, :])
    gate_now = gate[...]
    sig = sigmoid(gate_now)
    silu = gate_now * sig
    with_skip = y_in[...] + skip * inner
    gated = with_skip * silu
    ones = block_ones[...]
    scale = lax.rsqrt(split_nn(gated * gated, ones) * (1.0 / PD) + EPS)
    grad_now = grad[...]
    unit = gated * scale
    grad_unit = grad_now * gain
    mean = split_nn(grad_unit * unit, ones) * (1.0 / PD)
    grad_gated = scale * (grad_unit - unit * mean)
    grad_y = grad_gated * silu
    gy_out[...] = grad_y
    gate_out[...] = (grad_gated * with_skip * (sig * (1.0 + gate_now * (1.0 - sig)))).astype(BF16)
    params_out[0:1, :] += jnp.sum(grad_y * inner, axis=0, keepdims=True)
    params_out[1:2, :] += jnp.sum(grad_now * unit, axis=0, keepdims=True)
    inflow = jnp.where(start < 0, jnp.exp(cum_now + so_far[0:1, :]), 0.0)
    state_out[...] += low_tn(grad_y * split_nn(inflow, spread[...]), act[:, inner_width + NST :])
    so_far[...] = so_far[...] + jnp.broadcast_to(cum_now[rows - 1 : rows, :], so_far.shape)


def scan_back_kernel(
    docs,
    inner_width,
    meta,
    act,
    slope,
    step_in,
    sig_in,
    cum,
    grad_y_in,
    state_in,
    grad_end,
    mixed,
    edge,
    taps,
    heads,
    params,
    spread,
    spread_t,
    gmix_out,
    gstep_out,
    tail_out,
    edge_out,
    taps_out,
    heads_out,
    ext,
    grad_state,
):
    c = pl.num_programs(0) - 1 - pl.program_id(0)
    rows = act.shape[0]

    @pl.when(pl.program_id(0) == 0)
    def _():
        grad_state[...] = grad_end[...]
        ext[0:EDGE] = jnp.zeros((EDGE, ext.shape[1]), F32)
        ext[EDGE + rows :] = jnp.zeros((EDGE, ext.shape[1]), F32)
        taps_out[...] = jnp.zeros_like(taps_out)
        heads_out[...] = jnp.zeros_like(heads_out)

    @pl.when(pl.program_id(0) > 0)
    def _():
        ext[EDGE + rows :] = ext[EDGE : 2 * EDGE]

    at = c * rows
    row = at + iota((rows, 1), 0)
    start = start_of(row, meta, docs)
    last_start = start_of_one(at + rows - 1, meta, docs)
    inner = act[:, :inner_width]
    write = act[:, inner_width : inner_width + NST].astype(BF16)
    read = act[:, inner_width + NST :].astype(BF16)
    step = step_in[...]
    cum_now = cum[...]
    grad_y = grad_y_in[...]
    spread_now = spread[...]
    spread_back = spread_t[...]
    state = state_in[...]
    grads = grad_state[...]
    total = cum_now[rows - 1 : rows, :]
    step_wide = split_nn(step, spread_now)
    weighted = inner * step_wide
    tail = split_nn(jnp.where(row >= last_start, jnp.exp(total - cum_now), 0.0), spread_now)
    inflow = split_nn(jnp.where(start < at, jnp.exp(cum_now), 0.0), spread_now)
    kept_row = jnp.exp(total) * jnp.where(last_start < at, 1.0, 0.0)

    grads_low = grads.astype(BF16)
    state_low = state.astype(BF16)
    from_state = tail * product_nt(write, grads_low)
    leaving = split_nn(weighted * from_state, spread_back)
    grad_write = low_nn(tail * weighted, grads_low)
    arriving_y = inflow * grad_y
    arriving_low = arriving_y.astype(BF16)
    grad_read = product(arriving_low, state_low)
    arriving = split_nn(arriving_y * product_nt(read, state_low), spread_back)
    grad_state[...] = split_nt(
        spread_back, jnp.broadcast_to(kept_row, (NST, LANES))
    ) * grads + product_tn(arriving_low, read)
    both = split_nt(jnp.ones((8, NST), BF16), grads * state)
    kept_grad = kept_row * split_nn(both, spread_back)[0:1, :]
    grad_total = kept_grad + jnp.sum(leaving, axis=0, keepdims=True)

    couple_t = product_nt(write, read)
    at_key = iota((rows, rows), 0)
    at_query = iota((rows, rows), 1)
    end_row = at + iota((1, rows), 1)
    start_row = start_of(end_row, meta, docs) - at
    linked = (at_key >= start_row) & (at_key <= at_query)
    cum_t = cum_now.T
    lane = iota((rows, LANES), 1)
    sub = iota((LANES, rows), 0)
    weighted_low = weighted.astype(BF16)
    grad_y_low = grad_y.astype(BF16)
    grad_couple = jnp.zeros((rows, rows), F32)
    grad_cum = arriving - leaving
    grad_cum_t = jnp.zeros((LANES, rows), F32)
    pieces = []
    for pair in range(inner_width // LANES):
        span = slice(pair * LANES, (pair + 1) * LANES)
        values = weighted_low[:, span]
        grads_here = grad_y_low[:, span]
        results = []
        for side in range(2):
            head = 2 * pair + side
            arg = cum_t[head : head + 1, :] - cum_now[:, head : head + 1]
            decay = jnp.exp(jnp.where(linked, arg, MASKED))
            mine = jnp.where((lane >= PD) == (side == 1), values, jnp.zeros_like(values))
            grad_mixing = product_nt(mine, grads_here) * decay
            grad_couple = grad_couple + grad_mixing
            by_log = grad_mixing * couple_t
            grad_cum = grad_cum - jnp.where(
                lane == head, jnp.sum(by_log, axis=1, keepdims=True), 0.0
            )
            grad_cum_t = grad_cum_t + jnp.where(
                sub == head, jnp.sum(by_log, axis=0, keepdims=True), 0.0
            )
            results.append(product((couple_t * decay).astype(BF16), grads_here))
        pieces.append(jnp.where(lane < PD, results[0], results[1]))
    grad_weighted = jnp.concatenate(pieces, axis=1) + from_state
    grad_couple_low = grad_couple.astype(BF16)
    grad_write = grad_write + product(grad_couple_low, read)
    grad_read = grad_read + product_tn(grad_couple_low, write)

    grad_cum = grad_cum + grad_cum_t.T
    upper = (at_query >= at_key).astype(F32)
    grad_decay = (
        jnp.dot(upper, grad_cum, precision=HIGH, preferred_element_type=F32) + grad_total
    )
    rate = heads[1:2, :]
    grad_inner = grad_weighted * step_wide + grad_y * params[0:1, :]
    grad_step = split_nn(grad_weighted * inner, spread_back) - grad_decay * rate
    grad_raw = grad_step * sig_in[...]
    gstep_out[...] = grad_raw.astype(BF16)
    heads_out[0:1, :] += jnp.sum(grad_raw, axis=0, keepdims=True)
    heads_out[1:2, :] += jnp.sum(grad_decay * (-step * rate), axis=0, keepdims=True)

    grad_pre = jnp.concatenate([grad_inner, grad_write, grad_read], axis=1) * slope[...]
    ext[EDGE : EDGE + rows] = grad_pre
    taps_out[CONV : CONV + 1, :] += jnp.sum(grad_pre, axis=0, keepdims=True)
    mixed_now = mixed[...].astype(F32)
    grad_mixed = jnp.zeros_like(grad_pre)
    for lag in range(CONV):
        target = row + lag
        keep = (target - start_of(target, meta, docs) >= lag).astype(F32)
        moved = ext[EDGE + lag : EDGE + lag + rows] * keep
        grad_mixed = grad_mixed + taps[CONV - 1 - lag : CONV - lag, :] * moved
        taps_out[CONV - 1 - lag : CONV - lag, :] += jnp.sum(
            moved * mixed_now, axis=0, keepdims=True
        )
    gmix_out[...] = grad_mixed.astype(BF16)

    @pl.when(pl.program_id(0) == 0)
    def _():
        tail_out[...] = grad_mixed[rows - EDGE :]

    @pl.when(c == 0)
    def _():
        before = iota((EDGE, 1), 0) - EDGE
        edge_now = edge[...]
        grad_edge = jnp.zeros_like(edge_now)
        for lag in range(1, CONV):
            target = before + lag
            keep = (target - start_of(target, meta, docs) >= lag).astype(F32)
            moved = ext[lag : lag + EDGE] * keep
            grad_edge = grad_edge + taps[CONV - 1 - lag : CONV - lag, :] * moved
            taps_out[CONV - 1 - lag : CONV - lag, :] += jnp.sum(
                moved * edge_now, axis=0, keepdims=True
            )
        edge_out[...] = grad_edge


def call(kernel, grid, ins, outs, scratch=()):
    def spec(shape, block, index):
        if block == "smem":
            return pl.BlockSpec(memory_space=pltpu.SMEM)
        if block is None:
            return pl.BlockSpec(shape, lambda i: (0,) * len(shape))
        return pl.BlockSpec(block, index)

    return pl.pallas_call(
        kernel,
        grid=(grid,),
        in_specs=[spec(a.shape, block, index) for a, block, index in ins],
        out_specs=[spec(shape, block, index) for shape, _, block, index in outs],
        out_shape=[jax.ShapeDtypeStruct(shape, kind) for shape, kind, _, _ in outs],
        scratch_shapes=list(scratch),
        compiler_params=pltpu.CompilerParams(
            dimension_semantics=("arbitrary",), vmem_limit_bytes=VMEM_BYTES
        ),
    )(*[a for a, _, _ in ins])


def by_row(i):
    return (i, 0)


def chain(gathered, order, width, heads, reached):
    state = jnp.zeros((width, NST), F32)
    for k in order:
        own = gathered[k, :width].astype(F32)
        through = gathered[k, width].astype(F32) + gathered[k, width + 1].astype(F32)
        wide = jnp.repeat(through[:heads], PD)[:, None]
        state = jnp.where(reached(k), wide * state + own, state)
    return state


def rms_scale(values, gain):
    return values * lax.rsqrt(jnp.mean(values * values, axis=-1, keepdims=True) + EPS) * gain


def rms_back(values, gain, grad):
    scale = lax.rsqrt(jnp.mean(values * values, axis=-1, keepdims=True) + EPS)
    unit = values * scale
    inner = jnp.mean(grad * gain * values, axis=-1, keepdims=True)
    return (scale * (grad * gain - values * scale * scale * inner), jnp.sum(grad * unit, axis=0))


def body(
    tokens,
    cotangent,
    lengths,
    norm1_gain,
    norm2_gain,
    query_proj,
    keyval_proj,
    attn_proj,
    inner_proj,
    state_proj,
    step_proj,
    conv_inner,
    conv_state,
    step_bias,
    decay_log,
    skip_gain,
    mamba_gain,
    mamba_proj,
    gateup_proj,
    down_proj,
):
    rows = tokens.shape[0]
    rank = lax.axis_index("tp")
    ranks = lax.axis_size("tp")
    ctx_rank = lax.axis_index("ctx")
    ctx_size = lax.axis_size("ctx")
    pack = rows * ctx_size
    shard = query_proj.shape[0]
    width = inner_proj.shape[2]
    heads = width // PD
    mix = width + 2 * NST
    ff = gateup_proj.shape[2]
    docs = lengths.shape[1]
    quarter = rows // ranks
    chunks = rows // CHUNK
    kv_head = rank * (query_proj.shape[1] // HD) // (H // KVH)

    kv_shard = lax.dynamic_slice_in_dim(keyval_proj, kv_head * HD, HD, 2).reshape(shard, 2 * HD)
    step_shard = jnp.pad(step_proj, ((0, 0), (0, LANES - heads)))
    first_shard = jnp.concatenate(
        [
            inner_proj.reshape(shard, 2 * width),
            state_proj.reshape(shard, 2 * NST),
            query_proj,
            kv_shard,
            step_shard,
        ],
        axis=1,
    )
    mixer_shard = jnp.concatenate([attn_proj.T, mamba_proj.T], axis=1)
    first_w = lax.all_gather(first_shard, WEIGHT_AXES, axis=0, tiled=True)
    mixer_w = lax.all_gather(mixer_shard, WEIGHT_AXES, axis=0, tiled=True)
    gateup_w = lax.all_gather(
        gateup_proj.reshape(shard, 2 * ff), WEIGHT_AXES, axis=0, tiled=True
    )
    down_w = lax.all_gather(down_proj.T, WEIGHT_AXES, axis=0, tiled=True)

    first_row = ctx_rank * rows
    bounds = jnp.cumsum(lengths[0])
    starts = bounds - lengths[0] - first_row
    meta = jnp.concatenate([starts, first_row[None]]).astype(jnp.int32)
    local = jnp.arange(rows, dtype=jnp.int32)
    doc_start = jnp.max(
        jnp.where(local[:, None] >= starts[None, :], starts[None, :], starts[0]), axis=1
    )
    frequency = ROPE_BASE ** (-jnp.arange(HD // 2, dtype=F32) / (HD // 2))
    angles = (local - doc_start).astype(F32)[:, None] * jnp.tile(frequency, 4)[None, :]
    sign = jnp.where(jnp.arange(LANES) % HD < HD // 2, -1.0, 1.0).astype(F32)
    cosine = jnp.cos(angles)
    sine = jnp.sin(angles) * sign[None, :]

    def mine(values, size, axis):
        return lax.dynamic_slice_in_dim(values, rank * size, size, axis)

    taps = jnp.concatenate([mine(conv_inner, width, 1), conv_state.reshape(CONV + 1, -1)], axis=1)
    taps = jnp.pad(taps, ((0, 8 - (CONV + 1)), (0, 0)))
    bias = mine(step_bias, heads, 0)
    rate = jnp.exp(mine(decay_log, heads, 0))
    head_params = jnp.pad(jnp.stack([bias, rate]), ((0, 6), (0, LANES - heads)))
    params = jnp.pad(
        jnp.stack([jnp.repeat(mine(skip_gain, heads, 0), PD), mine(mamba_gain, width, 0)]),
        ((0, 6), (0, 0)),
    )
    channel_head = jnp.arange(width) // PD
    spread = (jnp.arange(LANES)[:, None] == channel_head[None, :]).astype(BF16)
    spread_t = spread.T
    block_ones = (channel_head[:, None] == channel_head[None, :]).astype(BF16)

    hidden_in = tokens.astype(F32)
    normed = rms_scale(hidden_in, norm1_gain).astype(BF16)
    onward = [(source, source + 1) for source in range(ctx_size - 1)]
    backward = [(source + 1, source) for source in range(ctx_size - 1)]
    edge_tokens = lax.ppermute(tokens[rows - EDGE :], "ctx", onward).astype(F32)
    edge_normed = rms_scale(edge_tokens, norm1_gain).astype(BF16)
    proj = product(normed, first_w)
    edge = product(edge_normed, first_w[:, width : width + mix]).astype(BF16).astype(F32)

    chunk_128 = (CHUNK, LANES)
    chunk_mix = (CHUNK, mix)
    chunk_width = (CHUNK, width)
    q_rot, kv_local, mixed, act, slope, step, sig, cum, state_local, end = call(
        functools.partial(prep_kernel, docs, width),
        chunks,
        [
            (meta, "smem", None),
            (proj, (CHUNK, proj.shape[1]), by_row),
            (edge, None, None),
            (taps, None, None),
            (head_params, None, None),
            (cosine, chunk_128, by_row),
            (sine, chunk_128, by_row),
            (spread, None, None),
            (spread_t, None, None),
        ],
        [
            ((rows, LANES), BF16, chunk_128, by_row),
            ((rows, LANES), BF16, chunk_128, by_row),
            ((rows, mix), BF16, chunk_mix, by_row),
            ((rows, mix), F32, chunk_mix, by_row),
            ((rows, mix), F32, chunk_mix, by_row),
            ((rows, LANES), F32, chunk_128, by_row),
            ((rows, LANES), F32, chunk_128, by_row),
            ((rows, LANES), F32, chunk_128, by_row),
            ((chunks * width, NST), F32, (width, NST), by_row),
            ((width + 16, NST), BF16, None, None),
        ],
        [
            pltpu.VMEM((CHUNK + EDGE, mix), F32),
            pltpu.VMEM((width, NST), F32),
            pltpu.VMEM((8, LANES), F32),
        ],
    )
    kv_all = lax.all_gather(kv_local, "ctx", axis=0, tiled=True)
    ends = lax.all_gather(end, "ctx")
    (y_intra,) = call(
        functools.partial(intra_kernel, docs, width),
        chunks,
        [
            (meta, "smem", None),
            (act, chunk_mix, by_row),
            (step, chunk_128, by_row),
            (cum, chunk_128, by_row),
            (spread, None, None),
        ],
        [((rows, width), F32, chunk_width, by_row)],
    )
    blocks = rows // QUERY_BLOCK
    block_128 = (QUERY_BLOCK, LANES)
    attended, lse = call(
        functools.partial(attend_kernel, docs),
        blocks,
        [(meta, "smem", None), (q_rot, block_128, by_row), (kv_all, None, None)],
        [((rows, LANES), BF16, block_128, by_row), ((rows, LANES), F32, block_128, by_row)],
    )
    state_in = chain(ends, range(ctx_size - 1), width, heads, lambda k: k < ctx_rank)
    mixer_low, y, states = call(
        functools.partial(finish_kernel, docs, width),
        chunks,
        [
            (meta, "smem", None),
            (y_intra, chunk_width, by_row),
            (act, chunk_mix, by_row),
            (cum, chunk_128, by_row),
            (proj, chunk_width, by_row),
            (attended, chunk_128, by_row),
            (state_local, (width, NST), by_row),
            (state_in, None, None),
            (params, None, None),
            (spread, None, None),
            (spread_t, None, None),
            (block_ones, None, None),
        ],
        [
            ((rows, LANES + width), BF16, (CHUNK, LANES + width), by_row),
            ((rows, width), F32, chunk_width, by_row),
            ((chunks * width, NST), F32, (width, NST), by_row),
        ],
        [pltpu.VMEM((width, NST), F32)],
    )

    def scatter_rows(values):
        return lax.psum_scatter(
            values.astype(BF16), "tp", scatter_dimension=0, tiled=True
        ).astype(F32)

    def gather_rows(values):
        return lax.all_gather(values, "tp", axis=0, tiled=True)

    hidden_q = mine(hidden_in, quarter, 0)
    residual = hidden_q + scatter_rows(product_nt(mixer_low, mixer_w))
    normed2 = gather_rows(rms_scale(residual, norm2_gain).astype(BF16))
    gateup = product(normed2, gateup_w)
    gate, up = (gateup[:, :ff], gateup[:, ff:])
    gate_sig = jax.nn.sigmoid(gate)
    gate_silu = gate * gate_sig
    hidden_act = (gate_silu * up).astype(BF16)
    grad_hidden = product(cotangent, down_w)
    grad_gateup = jnp.concatenate(
        [grad_hidden * up * (gate_sig * (1.0 + gate * (1.0 - gate_sig))), grad_hidden * gate_silu],
        axis=1,
    ).astype(BF16)
    grad_norm2 = scatter_rows(product_nt(grad_gateup, gateup_w))
    grad_values, norm2_part = rms_back(residual, norm2_gain, grad_norm2)
    grad_residual = mine(cotangent, quarter, 0).astype(F32) + grad_values
    grad_mix = gather_rows(grad_residual.astype(BF16))
    layer_q = residual + scatter_rows(product_nt(hidden_act, down_w))
    layer_out = gather_rows(layer_q.astype(BF16))

    def to_owner(values):
        return lax.psum_scatter(
            values.astype(BF16), WEIGHT_AXES, scatter_dimension=0, tiled=True
        ).astype(F32)

    gateup_grad = to_owner(product_tn(normed2, grad_gateup)).reshape(gateup_proj.shape)
    down_grad = to_owner(product_tn(cotangent, hidden_act)).T

    grad_mixer = product(grad_mix, mixer_w)
    mixer_grad = to_owner(product_tn(grad_mix, mixer_low))
    attn_grad = mixer_grad[:, :LANES].T
    mamba_grad = mixer_grad[:, LANES:].T
    grad_att = grad_mixer[:, :LANES]
    grad_mamba = grad_mixer[:, LANES:]
    grad_y, grad_gate, params_grad, grad_in = call(
        functools.partial(finish_back_kernel, docs, width),
        chunks,
        [
            (meta, "smem", None),
            (grad_mamba, chunk_width, by_row),
            (y, chunk_width, by_row),
            (act, chunk_mix, by_row),
            (cum, chunk_128, by_row),
            (proj, chunk_width, by_row),
            (params, None, None),
            (spread, None, None),
            (block_ones, None, None),
        ],
        [
            ((rows, width), F32, chunk_width, by_row),
            ((rows, width), BF16, chunk_width, by_row),
            ((8, width), F32, None, None),
            ((width, NST), F32, None, None),
        ],
        [pltpu.VMEM((8, LANES), F32)],
    )
    grad_ins = lax.all_gather(
        jnp.concatenate([grad_in.astype(BF16), end[width:]], axis=0), "ctx"
    )
    grad_query, grad_kv = call(
        functools.partial(attend_back_kernel, docs),
        blocks,
        [
            (meta, "smem", None),
            (q_rot, block_128, by_row),
            (kv_all, None, None),
            (grad_att, block_128, by_row),
            (attended, block_128, by_row),
            (lse, block_128, by_row),
            (cosine, block_128, by_row),
            (sine, block_128, by_row),
        ],
        [
            ((rows, LANES), BF16, block_128, by_row),
            ((pack, LANES), F32, None, None),
        ],
    )
    grad_kv = lax.psum_scatter(
        grad_kv.astype(BF16), "ctx", scatter_dimension=0, tiled=True
    ).astype(F32)
    grad_end = chain(
        grad_ins, range(ctx_size - 1, 0, -1), width, heads, lambda k: k > ctx_rank
    )

    def back_row(i):
        return (chunks - 1 - i, 0)

    grad_mixed, grad_step, grad_tail, grad_edge, taps_grad, heads_grad = call(
        functools.partial(scan_back_kernel, docs, width),
        chunks,
        [
            (meta, "smem", None),
            (act, chunk_mix, back_row),
            (slope, chunk_mix, back_row),
            (step, chunk_128, back_row),
            (sig, chunk_128, back_row),
            (cum, chunk_128, back_row),
            (grad_y, chunk_width, back_row),
            (states, (width, NST), back_row),
            (grad_end, None, None),
            (mixed, chunk_mix, back_row),
            (edge, None, None),
            (taps, None, None),
            (head_params, None, None),
            (params, None, None),
            (spread, None, None),
            (spread_t, None, None),
        ],
        [
            ((rows, mix), BF16, chunk_mix, back_row),
            ((rows, LANES), BF16, chunk_128, back_row),
            ((EDGE, mix), F32, None, None),
            ((EDGE, mix), F32, None, None),
            ((8, mix), F32, None, None),
            ((8, LANES), F32, None, None),
        ],
        [pltpu.VMEM((CHUNK + 2 * EDGE, mix), F32), pltpu.VMEM((width, NST), F32)],
    )
    edge_grad = lax.ppermute(grad_edge, "ctx", backward)
    grad_mixed = lax.dynamic_update_slice_in_dim(
        grad_mixed, (grad_tail + edge_grad).astype(BF16), rows - EDGE, 0
    )
    half = HD // 2
    swapped = jnp.concatenate([grad_kv[:, half:HD], grad_kv[:, :half], grad_kv[:, HD:]], axis=1)
    is_key = jnp.arange(LANES)[None, :] < HD
    grad_kv = jnp.where(is_key, grad_kv * cosine - swapped * sine, grad_kv).astype(BF16)

    grad_all = jnp.concatenate([grad_gate, grad_mixed, grad_query, grad_kv, grad_step], axis=1)
    grad_norm1 = scatter_rows(product_nt(grad_all, first_w))
    grad_values, norm1_part = rms_back(hidden_q, norm1_gain, grad_norm1)
    tokens_grad = gather_rows((grad_residual + grad_values).astype(BF16))
    first_grad = to_owner(product_tn(normed, grad_all))
    inner_grad = first_grad[:, : 2 * width].reshape(inner_proj.shape)
    base = width + mix
    query_grad = first_grad[:, base : base + LANES]
    step_grad = first_grad[:, base + 2 * LANES : base + 2 * LANES + heads]
    kv_wide = lax.dynamic_update_slice_in_dim(
        jnp.zeros(keyval_proj.shape, F32),
        first_grad[:, base + LANES : base + 2 * LANES].reshape(shard, 2, HD),
        kv_head * HD,
        2,
    )
    shared = jnp.concatenate(
        [kv_wide.reshape(shard, -1), first_grad[:, 2 * width : base]], axis=1
    )
    shared = lax.psum(shared, "tp")
    keyval_grad = shared[:, : 2 * KVH * HD].reshape(keyval_proj.shape)
    state_grad = shared[:, 2 * KVH * HD :].reshape(state_proj.shape)

    def spread_out(values, full_shape, size, axis):
        return lax.dynamic_update_slice_in_dim(
            jnp.zeros(full_shape, F32), values, rank * size, axis
        )

    small = lax.psum(
        (
            norm1_part,
            norm2_part,
            spread_out(taps_grad[: CONV + 1, :width], conv_inner.shape, width, 1),
            taps_grad[: CONV + 1, width:].reshape(conv_state.shape),
            spread_out(heads_grad[0, :heads], step_bias.shape, heads, 0),
            spread_out(heads_grad[1, :heads], decay_log.shape, heads, 0),
            spread_out(
                jnp.sum(params_grad[0].reshape(heads, PD), axis=1), skip_gain.shape, heads, 0
            ),
            spread_out(params_grad[1], mamba_gain.shape, width, 0),
        ),
        ("dp", "ctx", "tp"),
    )
    return (
        layer_out,
        tokens_grad,
        small[0],
        small[1],
        query_grad,
        keyval_grad,
        attn_grad,
        inner_grad,
        state_grad,
        step_grad,
        small[2],
        small[3],
        small[4],
        small[5],
        small[6],
        small[7],
        mamba_grad,
        gateup_grad,
        down_grad,
    )


def solution(mesh):
    rows_split = P(("dp", "ctx"), None)
    split_0 = P(("dp", "ctx"), "tp")
    split_0_whole = P(("dp", "ctx"), None, None)
    split_0_last = P(("dp", "ctx"), None, "tp")
    split_1 = P("tp", ("dp", "ctx"))
    return jax.shard_map(
        body,
        mesh=mesh,
        in_specs=(
            rows_split,
            rows_split,
            P("dp", None),
            P(),
            P(),
            split_0,
            split_0_whole,
            split_1,
            split_0_last,
            split_0_whole,
            split_0,
            P(),
            P(),
            P(),
            P(),
            P(),
            P(),
            split_1,
            split_0_last,
            split_1,
        ),
        out_specs=(
            rows_split,
            rows_split,
            P(),
            P(),
            split_0,
            split_0_whole,
            split_1,
            split_0_last,
            split_0_whole,
            split_0,
            P(),
            P(),
            P(),
            P(),
            P(),
            P(),
            split_1,
            split_0_last,
            split_1,
        ),
        check_vma=False,
    )
```

time: 1730 us -> 880 us (0.51)
  blocking collectives: 297 us -> 63 us
  matrix products: 269 us -> 62.4 us
  local copies, waits for them, and re-layouts: 225 us -> 59.4 us
  other arithmetic: 193 us -> 33.4 us
  waiting for transfers between devices: 687 us -> 569 us
  Pallas kernels: 0 us -> 58.2 us
  loops' own time: 18.8 us -> 0 us
    all_gather x12 -> x2, blocking collectives: 240 us -> 13.1 us  [the longest x1 7.37 us: body(): ends = lax.all_gather(end, 'ctx')]
    dot_general x96 -> x5, matrix products: 217 us -> 26.1 us  [product(): return jnp.dot(left, right, preferred_element_type=F32)]
    all_gather x3 -> x8, waiting for transfers between devices: 32.2 us -> 208 us  [the longest x4 79.2 us: gather_rows(): return lax.all_gather(values, 'tp', axis=0, tiled=True)]
    unnamed x13 -> x19, waiting for transfers between devices: 214 us -> 64.4 us
    psum x3 -> x1, waiting for transfers between devices: 118 us -> 0.01 us  [body(): shared = lax.psum(shared, 'tp')]
    dynamic_update_slice x28 -> x6, local copies, waits for them, and re-layouts: 86 us -> 4.85 us  [the longest x1 4.21 us: body(): lax.dynamic_update_slice_in_dim(jnp.zeros(keyval_proj.shape, F32), first_...]
    another operation x50 -> x3, other arithmetic: 69.4 us -> 0.2 us
    pallas_call x0 -> x7, Pallas kernels: none -> 58.2 us  [call(): pl.pallas_call(kernel, grid=(grid,), in_specs=[spec(a.shape, block, index...]
  transfers between devices with their start and end apart: 14 -> 20, of which waited for: 11 -> 16; matrix products, arithmetic and copies ran while one was open for 23% -> 10% of each run, Pallas kernels for 0% -> 5%
where the time goes in v1:
time: 880 us; the launch traced here: 868 us
  waiting for transfers between devices  569 us (65%)
  blocking collectives  63 us (7%)
  matrix products  62.4 us (7%)
  local copies, waits for them, and re-layouts  59.4 us (7%)
  Pallas kernels  58.2 us (7%)
  other arithmetic  33.4 us (4%)
  between operations  15.3 us (2%)
    reduce_scatter x3, waiting for transfers between devices, to_owner(): lax.psum_scatter(values.astype(BF16), WEIGHT_AXES, scatter_dimension=0, t...  205 us
    reduce_scatter x4, waiting for transfers between devices, scatter_rows(): lax.psum_scatter(values.astype(BF16), 'tp', scatter_dimension=0, tiled=True)  88.1 us
    all_gather x4, waiting for transfers between devices, gather_rows(): return lax.all_gather(values, 'tp', axis=0, tiled=True)  79.2 us
    unnamed x19, waiting for transfers between devices  64.4 us
    pallas_call x7, Pallas kernels, call(): pl.pallas_call(kernel, grid=(grid,), in_specs=[spec(a.shape, block, index...  58.2 us
    all_gather x1, waiting for transfers between devices, body(): first_w = lax.all_gather(first_shard, WEIGHT_AXES, axis=0, tiled=True)  48 us
    all_gather x1, waiting for transfers between devices, body(): lax.all_gather(gateup_proj.reshape(shard, 2 * ff), WEIGHT_AXES, axis=0, t...  46.2 us
    psum x1, blocking collectives, body(): lax.psum((norm1_part, norm2_part, spread_out(taps_grad[:CONV + 1, :width]...  41.7 us
  transfers between devices with their start and end apart: 20, of which 16 were waited for; matrix products, arithmetic and copies ran while one was open for 10% of the time, Pallas kernels for 5%

profile of v1, /device:TPU:0, one launch (start us, length us, event | category | flops | bytes accessed | tf_op | source)
XLA Modules:
  0.0 868.4 jit_solution(3568263839586162886)
XLA Ops:
  25.2 48.0 %all-gather.11.cloned.1.call-done = bf16[1024,1408]{1,0:T(8,128)(2,1)} async-done(((bf16[128,1408]{1,0:T(8,128)(2,1)}), bf16[1024,1408]{1,0:T(8,128)(2,1)}) %all-gather.11.cloned.1.call-update) | async-done | bytes 2883600 | tf_op jit(solution)/shard_map/all_gather | solution.py:674
  74.8 8.4 fusion.23.proj.gate
  83.3 10.7 %shard_map.339 = (bf16[1024,128]{1,0:T(8,128)(2,1)S(1)}, bf16[1024,128]{1,0:T(8,128)(2,1)S(1)}, bf16[1024,640]{1,0:T(8,128)(2,1)S(1)}, f32[1024,640]{1,0:T(8,128...) custom-call(s32[5]{0:T(128)S(1)} %pad_add_fusion.meta, ...), custom_call_target="tpu_custom_call" | custom-call | tf_op jit(solution)/shard_map/pallas_call | solution.py:585
  97.4 7.4 all-gather
  105.5 8.3 all_gather.40.kv
  147.6 27.4 %reduce-scatter.12.cloned.1.call-done = bf16[256,1024]{1,0:T(8,128)(2,1)} async-done(((bf16[1024,1024]{1,0:T(8,128)(2,1)}), bf16[256,1024]{1,0:T(8,128)(2,1)}) %reduce-scatter.12.cloned.1.call-update) | async-done | bytes 524304 | tf_op jit(solution)/shard_map/reduce_scatter | solution.py:805
  180.9 46.2 %all-gather.17.cloned.1.call-done = bf16[1024,1024]{1,0:T(8,128)(2,1)} async-done(((bf16[128,1024]{1,0:T(8,128)(2,1)}), bf16[1024,1024]{1,0:T(8,128)(2,1)}) %all-gather.17.cloned.1.call-update) | async-done | bytes 2097168 | tf_op jit(solution)/shard_map/all_gather | solution.py:676
  227.1 23.2 %all-gather.15.cloned.1.call-done = bf16[1024,1024]{1,0:T(8,128)(2,1)} async-done(((bf16[256,1024]{1,0:T(8,128)(2,1)}), bf16[1024,1024]{1,0:T(8,128)(2,1)}) %all-gather.15.cloned.1.call-update) | async-done | bytes 2097168 | tf_op jit(solution)/shard_map/all_gather | solution.py:810
  250.3 6.7 fusion.54
  256.9 35.0 %all-gather.19.cloned.1.call-done = bf16[1024,512]{0,1:T(8,128)(2,1)} async-done(((bf16[128,512]{0,1:T(8,128)(2,1)}), bf16[1024,512]{0,1:T(8,128)(2,1)}) %all-gather.19.cloned.1.call-update) | async-done | bytes 1048592 | tf_op jit(solution)/shard_map/all_gather | solution.py:679
  303.7 30.0 %reduce-scatter.16.cloned.1.call-done = bf16[256,1024]{1,0:T(8,128)(2,1)} async-done(((bf16[1024,1024]{1,0:T(8,128)(2,1)}), bf16[256,1024]{1,0:T(8,128)(2,1)}) %reduce-scatter.16.cloned.1.call-update) | async-done | bytes 524304 | tf_op jit(solution)/shard_map/reduce_scatter | solution.py:805
  340.5 21.6 %all-gather.23.cloned.1.call-done = bf16[1024,1024]{1,0:T(8,128)(2,1)} async-done(((bf16[256,1024]{1,0:T(8,128)(2,1)}), bf16[1024,1024]{1,0:T(8,128)(2,1)}) %all-gather.23.cloned.1.call-update) | async-done | bytes 2097168 | tf_op jit(solution)/shard_map/all_gather | solution.py:810
  365.5 6.6 shard_map.343
  378.9 9.1 %shard_map.345 = (bf16[1024,128]{1,0:T(8,128)(2,1)S(1)}, f32[2048,128]{1,0:T(8,128)S(1)}) custom-call(s32[5]{0:T(128)S(1)} %pad_add_fusion.meta, bf16[1024,128]{1,0:T(8,128)(2,1)S(1)} %copy-done.10, bf16[2048,128]{1,0:T(8,128)(2,1)S(1)} %all_gather.40.kv, f32[1024,128]{1,0:T(8,128)S(1)} %slice.148.grad, bf16[1024,128]{1,0:T(8,128)(2,1)S(1)} %get-tuple-element.51.att, ...), custom_call_target="tpu_custom_call" | custom-call | tf_op jit(solution)/shard_map/pallas_call | solution.py:585
  392.4 16.8 %shard_map.344 = (bf16[1024,640]{1,0:T(8,128)(2,1)S(1)}, bf16[1024,128]{1,0:T(8,128)(2,1)S(1)}, f32[8,640]{1,0:T(8,128)S(1)}, f32[8,640]{1,0:T(8,128)S(1)}, f32[8,640]{1,0:T(8,128)S(1)}, /*index=5*/f32[8,128]{1,0:T(8,128)S(1)}) custom-call(s32[5]{0:T(128)S(1)} %pad_add_fusion.meta, f32[1024,640]{1,0:T(8,128)} %get-tuple-element.46.act, ...), custom_call_target="tpu_custom_call" | custom-call | tf_op jit(solution)/shard_map/pallas_call | solution.py:585
  430.2 6.8 convolution_convert_fusion
  463.3 73.7 %reduce-scatter.22.cloned.1.call-done = bf16[128,1408]{1,0:T(8,128)(2,1)} async-done(((bf16[1024,1408]{1,0:T(8,128)(2,1)}), bf16[128,1408]{1,0:T(8,128)(2,1)}) %reduce-scatter.22.cloned.1.call-update) | async-done | bytes 360464 | tf_op jit(solution)/shard_map/reduce_scatter | solution.py:833
  544.6 26.3 %reduce-scatter.14.cloned.1.call-done = bf16[256,1024]{1,0:T(8,128)(2,1)} async-done(((bf16[1024,1024]{1,0:T(8,128)(2,1)}), bf16[256,1024]{1,0:T(8,128)(2,1)}) %reduce-scatter.14.cloned.1.call-update) | async-done | bytes 524304 | tf_op jit(solution)/shard_map/reduce_scatter | solution.py:805
  575.0 63.0 %reduce-scatter.28.cloned.1.call-done = bf16[128,512]{1,0:T(8,128)(2,1)} async-done(((bf16[1024,512]{1,0:T(8,128)(2,1)}), bf16[128,512]{1,0:T(8,128)(2,1)}) %reduce-scatter.28.cloned.1.call-update) | async-done | bytes 131088
  639.8 68.6 %reduce-scatter.26.cloned.1.call-done = bf16[128,1024]{1,0:T(8,128)(2,1)} async-done(((bf16[1024,1024]{1,0:T(8,128)(2,1)}), bf16[128,1024]{1,0:T(8,128)(2,1)}) %reduce-scatter.26.cloned.1.call-update) | async-done | bytes 262160 | tf_op jit(solution)/shard_map/reduce_scatter | solution.py:833
  711.5 62.6 %reduce-scatter.24.cloned.1.call-done = bf16[128,512]{1,0:T(8,128)(2,1)} async-done(((bf16[1024,512]{1,0:T(8,128)(2,1)}), bf16[128,512]{1,0:T(8,128)(2,1)}) %reduce-scatter.24.cloned.1.call-update) | async-done | bytes 131088 | tf_op jit(solution)/shard_map/reduce_scatter | solution.py:833
  776.6 41.7 %all-reduce.4 = (f32[1024]{0:T(1024)}, f32[1024]{0:T(1024)}, f32[5,1536]{1,0:T(8,128)}, f32[5,2,128]{2,1,0:T(2,128)}, f32[24]{0:T(128)}, /*index=5*/f32[24]{0:T(128)}, f32[24]{0:T(128)}, f32[1536]{0:T(1024)}) all-reduce(f32[1024]{0:T(1024)S(1)} %get-tuple-element.149, ...), channel_id=1, replica_groups=mesh['dp'=4,'ctx'=2,'tp'=4] {'dp','ctx','tp'}, use_global_device_ids=true, to_apply=%region_14.15 | all-reduce | flops 12616 | bytes 100928 | tf_op jit(solution)/shard_map/psum | solution.py:966
  822.4 9.8 %all-gather.21.cloned.1.call-done = bf16[1024,1024]{1,0:T(8,128)(2,1)} async-done(((bf16[256,1024]{1,0:T(8,128)(2,1)}), bf16[1024,1024]{1,0:T(8,128)(2,1)}) %all-gather.21.cloned.1.call-update) | async-done | bytes 2097168 | tf_op jit(solution)/shard_map/all_gather | solution.py:810
  832.2 24.6 %all-gather.25.cloned.1.call-done = bf16[1024,1024]{1,0:T(8,128)(2,1)} async-done(((bf16[256,1024]{1,0:T(8,128)(2,1)}), bf16[1024,1024]{1,0:T(8,128)(2,1)}) %all-gather.25.cloned.1.call-update) | async-done | bytes 2097168 | tf_op jit(solution)/shard_map/all_gather | solution.py:810
  (296 shorter events, 170.6 us)
Async XLA Ops:
  7.2 66.0 %all-gather.11.cloned.1.call-start = ((), (), s32[]{:S(2)}) async-start(), calls=%async_computation.9 | async-start | bytes 3244032 | tf_op jit(solution)/shard_map/all_gather | solution.py:674
  12.7 124.9 %all-gather.13.cloned.1.call-start = ((), (), s32[]{:S(2)}) async-start(), calls=%async_computation.10 | async-start | bytes 1179648 | tf_op jit(solution)/shard_map/all_gather | solution.py:675
  13.5 11.6 %collective-permute-start = (bf16[8,1024]{1,0:T(8,128)(2,1)S(1)}, bf16[8,1024]{1,0:T(8,128)(2,1)S(1)}, u32[]{:S(2)}, u32[]{:S(2)}) collective-permute-start(bf16[8,1024]{1,0:T(8,128)(2,1)S(1)} %slice.104), channel_id=1, source_target_pairs={{0,4},{1,5},{2,6},{3,7},{8,12},{9,13},{10,14},{11,15},{16,20},{17,... | collective-permute-start | bytes 49160 | tf_op jit(solution)/shard_map/ppermute | solution.py:716
  19.9 155.1 %reduce-scatter.12.cloned.1.call-start = ((), (), s32[]{:S(2)}) async-start(), calls=%async_computation.11 | async-start | bytes 2621440 | tf_op jit(solution)/shard_map/reduce_scatter | solution.py:805
  141.7 85.4 %all-gather.17.cloned.1.call-start = ((), (), s32[]{:S(2)}) async-start(), calls=%async_computation.13 | async-start | bytes 2359296 | tf_op jit(solution)/shard_map/all_gather | solution.py:676
  143.5 106.8 %all-gather.15.cloned.1.call-start = ((), (), s32[]{:S(2)}) async-start(), calls=%async_computation.12 | async-start | bytes 2621440 | tf_op jit(solution)/shard_map/all_gather | solution.py:810
  180.3 111.6 %all-gather.19.cloned.1.call-start = ((), (), s32[]{:S(2)}) async-start(), calls=%async_computation.14 | async-start | bytes 1179648 | tf_op jit(solution)/shard_map/all_gather | solution.py:679
  180.9 152.9 %reduce-scatter.16.cloned.1.call-start = ((), (), s32[]{:S(2)}) async-start(), calls=%async_computation.17 | async-start | bytes 2621440 | tf_op jit(solution)/shard_map/reduce_scatter | solution.py:805
  303.3 58.8 %all-gather.23.cloned.1.call-start = ((), (), s32[]{:S(2)}) async-start(), calls=%async_computation.18 | async-start | bytes 2621440 | tf_op jit(solution)/shard_map/all_gather | solution.py:810
  339.3 77.6 %reduce-scatter.18.cloned.1.call-start = ((), (), s32[]{:S(2)}) async-start(), calls=%async_computation.19 | async-start | bytes 786432 | tf_op jit(solution)/shard_map/reduce_scatter | solution.py:889
  389.0 72.5 %reduce-scatter.20.cloned.1.call-start = ((), (), s32[]{:S(2)}) async-start(), calls=%async_computation.20 | async-start | bytes 2621440 | tf_op jit(solution)/shard_map/reduce_scatter | solution.py:805
  409.2 5.7 collective-permute-start.1
  428.7 108.4 %reduce-scatter.22.cloned.1.call-start = ((), (), s32[]{:S(2)}) async-start(), calls=%async_computation.22 | async-start | bytes 3244032 | tf_op jit(solution)/shard_map/reduce_scatter | solution.py:833
  437.1 133.8 %reduce-scatter.14.cloned.1.call-start = ((), (), s32[]{:S(2)}) async-start(), calls=%async_computation.15 | async-start | bytes 2621440 | tf_op jit(solution)/shard_map/reduce_scatter | solution.py:805
  441.6 196.4 %reduce-scatter.28.cloned.1.call-start = ((), (), s32[]{:S(2)}) async-start(), calls=%async_computation.26 | async-start | bytes 1179648
  445.9 262.4 %reduce-scatter.26.cloned.1.call-start = ((), (), s32[]{:S(2)}) async-start(), calls=%async_computation.25 | async-start | bytes 2359296 | tf_op jit(solution)/shard_map/reduce_scatter | solution.py:833
  451.9 322.2 %reduce-scatter.24.cloned.1.call-start = ((), (), s32[]{:S(2)}) async-start(), calls=%async_computation.24 | async-start | bytes 1179648 | tf_op jit(solution)/shard_map/reduce_scatter | solution.py:833
  457.0 113.9 %copy-start.26 = (bf16[256,1024]{1,0:T(8,128)(2,1)S(1)}, bf16[256,1024]{1,0:T(8,128)(2,1)}, u32[]{:S(2)}) copy-start(bf16[256,1024]{1,0:T(8,128)(2,1)} %reduce-scatter.16.cloned.1.call-done) | copy-start | bytes 1572868
  457.0 113.9 %copy-start.39 = (f32[256]{0:T(256)S(1)}, f32[256]{0:T(256)}, u32[]{:S(2)}) copy-start(f32[256]{0:T(256)} %copy-done.38) | copy-start | bytes 3076
  457.0 363.0 %all-reduce.7.cloned.1.call-start = ((), (), s32[]{:S(2)}) async-start(), calls=%async_computation.23 | async-start | bytes 524288 | tf_op jit(solution)/shard_map/psum | solution.py:957
  544.5 287.7 %all-gather.21.cloned.1.call-start = ((), (), s32[]{:S(2)}) async-start(), calls=%async_computation.16 | async-start | bytes 2621440 | tf_op jit(solution)/shard_map/all_gather | solution.py:810
  574.3 202.3 %copy-start.36 = (f32[1024]{0:T(1024)S(1)}, f32[1024]{0:T(1024)}, u32[]{:S(2)}) copy-start(f32[1024]{0:T(1024)} %get-tuple-element.151) | copy-start | bytes 12292
  574.3 244.0 %copy-start.29 = (bf16[128,1408]{1,0:T(8,128)(2,1)S(1)}, bf16[128,1408]{1,0:T(8,128)(2,1)}, u32[]{:S(2)}) copy-start(bf16[128,1408]{1,0:T(8,128)(2,1)} %reduce-scatter.22.cloned.1.call-done) | copy-start | bytes 1081348
  574.4 282.4 %all-gather.25.cloned.1.call-start = ((), (), s32[]{:S(2)}) async-start(), calls=%async_computation.21 | async-start | bytes 2621440 | tf_op jit(solution)/shard_map/all_gather | solution.py:810
  (55 other events, 599.2 us)
Sparse Core Ops, SparseCore 0:
  12.8 60.3 all-gather.10
  75.8 40.6 all-gather.12
  141.8 33.1 reduce-scatter.11
  177.8 49.2 all-gather.16
  229.1 21.0 all-gather.14
  252.4 39.5 all-gather.18
  303.4 30.3 reduce-scatter.15
  339.4 22.5 all-gather.22
  389.1 17.8 reduce-scatter.17
  428.8 32.6 reduce-scatter.19
  465.1 71.9 reduce-scatter.21
  540.0 30.8 reduce-scatter.13
  574.7 63.2 reduce-scatter.27
  641.4 66.8 reduce-scatter.25
  711.6 62.4 reduce-scatter.23
  776.4 31.1 all-reduce.6
  809.6 22.5 all-gather.20
  834.2 22.5 all-gather.24
